TPU v7x, 128 devices: a whole 4x4x4 slice. The times are simulated.
128 devices in a mesh: ctx: 16 (over y, z_hi, core), tp: 8 (over x, z_lo).
Axes of the slice: x: 4, y: 4, z: 4 (z_hi: 2, z_lo: 2; z = z_hi * 2 + z_lo), core: 2. Of those that a mesh axis runs over, the one named last changes fastest.
Arguments:
- query: bfloat16 [2048, 64, 576], P('ctx', 'tp')
- latent: bfloat16 [2048, 576], P('ctx')
- d_out: bfloat16 [2048, 64, 512], P('ctx', 'tp'), may hold values from -1.5 to 1.5
- positions: int32 [2048], P('ctx'), may hold values from 0 to 2047, as said below
- doc_ids: int32 [2048], replicated, may hold values from 0 to 3, never falling along the last dimension, each value on 1 to 1024 neighbouring positions
Outputs:
- d_query: bfloat16 [2048, 64, 576], P('ctx', 'tp')
- d_latent: bfloat16 [2048, 576], P('ctx')
Inputs may be any that keep to these rules, and one draw needn't show every extreme that they name: A permutation; the rows of each index d of ctx hold two runs of 64 consecutive increasing positions: run b and the mirrored run counted from the end, b differing between indices.
All inputs are finite; a program needn't handle non-finite values.
Results may differ from a plain program's by a relative error of at most 0.024.
Values may be sent and summed in bfloat16 or wider, within the bound.
A program may use at most 128 MiB of HBM per device.

v0:
```python
import math

import jax
import jax.numpy as jnp
from jax import lax
from jax.sharding import PartitionSpec as P

SCALE = 192.0 ** (-0.5)


def contract_last(left, right):
    return lax.dot_general(
        left, right, (((1,), (1,)), ((), ())), preferred_element_type=jnp.float32
    )


def contract_first(left, right):
    return lax.dot_general(
        left, right, (((0,), (0,)), ((), ())), preferred_element_type=jnp.float32
    )


def block_spans(count):
    size = math.gcd(count, 512)
    return [(index * size, size) for index in range(count // size)]


def local(query, latent, d_out, positions, doc_ids):
    tok, heads, width = query.shape
    lat = d_out.shape[2]
    rows = tok * heads
    qflat = query.reshape(rows, width)
    gflat = d_out.reshape(rows, lat)
    my_docs = doc_ids[positions]
    tokens_all = tok * lax.axis_size("ctx")

    def token_mask(key_pos):
        key_docs = doc_ids[key_pos]
        return (key_pos[None, :] <= positions[:, None]) & (key_docs[None, :] == my_docs[:, None])

    def row_mask(mask):
        return jnp.broadcast_to(mask[:, None, :], (tok, heads, mask.shape[1])).reshape(
            rows, mask.shape[1]
        )

    def guarded(step, carry, keys, key_pos, first):
        mask = token_mask(key_pos)
        return step(carry, keys, mask, first)

    def forward_block(carry, keys, mask, first):
        peak, total, acc = carry
        allow = row_mask(mask)
        score = SCALE * contract_last(qflat, keys)
        masked = jnp.where(allow, score, jnp.float32(-1e30))
        new_peak = jnp.maximum(peak, jnp.max(masked, axis=1))
        weights = jnp.where(allow, jnp.exp(masked - new_peak[:, None]), jnp.float32(0.0))
        fade = jnp.exp(peak - new_peak)
        total = total * fade + jnp.sum(weights, axis=1)
        acc = acc * fade[:, None] + jnp.dot(
            weights.astype(jnp.bfloat16), keys[:, :lat], preferred_element_type=jnp.float32
        )
        return (new_peak, total, acc)

    stats_init = (
        jnp.full((rows,), -1e30, jnp.float32),
        jnp.zeros((rows,), jnp.float32),
        jnp.zeros((rows, lat), jnp.float32),
    )
    carry = stats_init
    start = jnp.int32(0)
    keys = lax.all_gather(latent, "ctx", axis=0, tiled=True)
    key_pos = lax.all_gather(positions, "ctx", axis=0, tiled=True)
    for offset, size in block_spans(keys.shape[0]):
        carry = guarded(
            forward_block,
            carry,
            keys[offset : offset + size],
            key_pos[offset : offset + size],
            start + offset,
        )
    peak, total, acc = carry
    out = (acc / total[:, None]).astype(jnp.bfloat16)
    lse = peak + jnp.log(total)
    delta = jnp.sum(gflat.astype(jnp.float32) * out.astype(jnp.float32), axis=1)

    def backward_block(carry, keys, mask, first):
        dq, dkv = carry
        allow = row_mask(mask)
        score = SCALE * contract_last(qflat, keys)
        prob = jnp.exp(jnp.where(allow, score - lse[:, None], jnp.float32(-1e30)))
        grad_p = contract_last(gflat, keys[:, :lat])
        grad_s = (prob * (grad_p - delta[:, None])).astype(jnp.bfloat16)
        dq = dq + SCALE * jnp.dot(grad_s, keys, preferred_element_type=jnp.float32)
        dkeys = SCALE * contract_first(grad_s, qflat)
        dvals = contract_first(prob.astype(jnp.bfloat16), gflat)
        dkeys = dkeys + jnp.pad(dvals, ((0, 0), (0, width - lat)))
        older = lax.dynamic_slice_in_dim(dkv, first, keys.shape[0], 0)
        dkv = lax.dynamic_update_slice_in_dim(dkv, older + dkeys, first, 0)
        return (dq, dkv)

    grads_init = (
        jnp.zeros((rows, width), jnp.float32),
        jnp.zeros((tokens_all, width), jnp.float32),
    )
    carry = grads_init
    start = jnp.int32(0)
    keys = lax.all_gather(latent, "ctx", axis=0, tiled=True)
    key_pos = lax.all_gather(positions, "ctx", axis=0, tiled=True)
    for offset, size in block_spans(keys.shape[0]):
        carry = guarded(
            backward_block,
            carry,
            keys[offset : offset + size],
            key_pos[offset : offset + size],
            start + offset,
        )
    dq, dkv = carry
    owned = lax.psum_scatter(dkv, "ctx", scatter_dimension=0, tiled=True)
    d_latent = lax.psum(owned, "tp").astype(jnp.bfloat16)
    d_query = dq.reshape(tok, heads, width).astype(jnp.bfloat16)
    return (d_query, d_latent)


def solution(mesh):
    return jax.shard_map(
        local,
        mesh=mesh,
        in_specs=(P("ctx", "tp", None), P("ctx", None), P("ctx", "tp", None), P("ctx"), P()),
        out_specs=(P("ctx", "tp", None), P("ctx", None)),
        check_vma=False,
    )
```

profile of v0, /device:TPU:0, one launch (start us, length us, event | category | flops | bytes accessed | tf_op | source)
XLA Modules:
  0.0 226.3 jit_solution(1680111148939097103)
XLA Ops:
  8.0 25.4 %all-gather = s32[16,1,128]{2,1,0:T(1,128)S(1)} all-gather(s32[1,1,128]{2,1,0:T(1,128)} %bitcast.74), channel_id=1, replica_groups=mesh['ctx'=16,'tp'=8] {'ctx'}, dimensions={0}, use_global_device_ids=true | all-gather | bytes 8704 | tf_op jit(solution)/shard_map/all_gather | solution.py:108
  33.4 3.1 %gather_fusion = s32[512]{0:T(512)S(1)} fusion(s32[2048]{0:T(1024)S(1)} %copy-done, s32[1024]{0:T(1024)S(1)} %pad_clamp_fusion.4), kind=kCustom, calls=%fused_computation | custom fusion | bytes 6144 | tf_op jit(solution)/shard_map/gather | solution.py:38
  36.6 3.1 %gather_fusion.2 = s32[512]{0:T(512)S(1)} fusion(s32[2048]{0:T(1024)S(1)} %copy-done, s32[1024]{0:T(1024)S(1)} %pad_clamp_fusion.2), kind=kCustom, calls=%fused_computation.2 | custom fusion | bytes 6144 | tf_op jit(solution)/shard_map/gather | solution.py:38
  39.8 3.1 %gather_fusion.3 = s32[512]{0:T(512)S(1)} fusion(s32[2048]{0:T(1024)S(1)} %copy-done, s32[1024]{0:T(1024)S(1)} %pad_clamp_fusion.1), kind=kCustom, calls=%fused_computation.3 | custom fusion | bytes 6144 | tf_op jit(solution)/shard_map/gather | solution.py:38
  42.9 3.1 %gather_fusion.4 = s32[512]{0:T(512)S(1)} fusion(s32[2048]{0:T(1024)S(1)} %copy-done, s32[1024]{0:T(1024)S(1)} %pad_clamp_fusion), kind=kCustom, calls=%fused_computation.4 | custom fusion | bytes 6144 | tf_op jit(solution)/shard_map/gather | solution.py:38
  46.1 1.1 gather_fusion.1
  48.2 1.4 copy.42
  49.6 1.3 copy.33
  52.8 1.4 copy.36
  54.3 1.3 copy.43
  55.6 8.0 %all-gather.3.cloned.1.call-done = bf16[2048,576]{0,1:T(8,128)(2,1)} async-done(((bf16[128,576]{0,1:T(8,128)(2,1)}), bf16[2048,576]{0,1:T(8,128)(2,1)}) %all-gather.3.cloned.1.call-update) | async-done | bytes 2359312 | tf_op jit(solution)/shard_map/all_gather | solution.py:107
  63.6 2.5 %fusion = (f32[1024]{0:T(1024)S(1)}, f32[1024,512]{0,1:T(8,128)S(1)}) fusion(pred[1024,512]{0,1:T(32,128)(4,1)} %copy.42, bf16[2048,576]{0,1:T(8,128)(2,1)} %all-gather.3.cloned.1.call-done, bf16[128,8,576]{2,1,0:T(8,128)(2,1)S(1)} %copy.33), kind=kOutput, calls=%fused_computation.24 | convolution fusion | flops 605551616 | bytes 4395008 | tf_op jit(solution)/shard_map/dot_general | solution.py:12
  67.2 1.1 fusion.3
  76.9 1.2 fusion.40
  79.4 1.7 multiply_reduce_fusion
  84.0 2.7 %dynamic_update_slice.12 = f32[2048,576]{0,1:T(8,128)} pad(f32[512,576]{0,1:T(8,128)S(1)} %fusion.12, f32[]{:T(128)} %constant.14.clone.1), padding=0_1536x0_0 | pad | bytes 5898244 | tf_op jit(solution)/shard_map/dynamic_update_slice | solution.py:98
  87.9 1.9 fusion.11
  90.9 3.6 %fusion.9 = f32[2048,576]{0,1:T(8,128)} fusion(f32[2048,576]{0,1:T(8,128)} %fusion.11, bf16[1024,512]{0,1:T(8,128)(2,1)S(1)} %multiply_convert_fusion.2, bf16[128,8,576]{2,1,0:T(8,128)(2,1)S(1)} %copy.33, f32[512,512]{0,1:T(8,128)S(1)} %fusion.46), kind=kOutput, calls=%fused_computation.35 | convolution fusion | flops 604864512 | bytes 5636096 | tf_op jit(solution)/shard_map/dot_general | solution.py:18
  96.6 3.2 %fusion.6 = f32[2048,576]{0,1:T(8,128)} fusion(f32[2048,576]{0,1:T(8,128)} %fusion.9, bf16[1024,512]{0,1:T(8,128)(2,1)S(1)} %multiply_convert_fusion.1, bf16[128,8,576]{2,1,0:T(8,128)(2,1)S(1)} %copy.33, f32[512,512]{0,1:T(8,128)S(1)} %fusion.44), kind=kOutput, calls=%fused_computation.31 | convolution fusion | flops 604864512 | bytes 5636096 | tf_op jit(solution)/shard_map/dot_general | solution.py:18
  99.9 1.2 copy-done.9
  105.5 2.0 multiply_convert_fusion
  108.3 1.8 copy.52
  110.0 71.4 %reduce-scatter.2.cloned.1.call-done = f32[128,576]{0,1:T(8,128)} async-done(((f32[2048,576]{0,1:T(8,128)}), f32[128,576]{0,1:T(8,128)}) %reduce-scatter.2.cloned.1.call-update) | async-done | bytes 294928 | tf_op jit(solution)/shard_map/reduce_scatter | solution.py:118
  181.5 38.1 %all-reduce.6 = bf16[128,576]{0,1:T(8,128)(2,1)} all-reduce(f32[128,576]{0,1:T(8,128)} %reduce-scatter.2.cloned.1.call-done), channel_id=1, replica_groups=mesh['ctx'=16,'tp'=8] {'tp'}, use_global_device_ids=true, to_apply=%region_10.11 | all-reduce | flops 73728 | bytes 442368 | tf_op jit(solution)/shard_map/psum | solution.py:119
  (76 shorter events, 26.8 us)
Async XLA Ops:
  7.2 26.2 %copy-start = (s32[2048]{0:T(1024)S(1)}, s32[2048]{0:T(1024)}, u32[]{:S(2)}) copy-start(s32[2048]{0:T(1024)} %param.9) | copy-start | bytes 24580
  7.2 56.4 %all-gather.3.cloned.1.call-start = ((), (), s32[]{:S(2)}) async-start(), calls=%async_computation.1 | async-start | bytes 2506752 | tf_op jit(solution)/shard_map/all_gather | solution.py:107
  7.9 173.5 %reduce-scatter.2.cloned.1.call-start = ((), (), s32[]{:S(2)}) async-start(), calls=%async_computation.2 | async-start | bytes 5013504 | tf_op jit(solution)/shard_map/reduce_scatter | solution.py:118
  39.7 6.4 %copy-start.16 = (s32[128]{0:T(128)S(1)}, s32[128]{0:T(128)}, u32[]{:S(2)}) copy-start(s32[128]{0:T(128)} %param.8) | copy-start | bytes 1540
  42.9 6.7 %copy-start.14 = (bf16[128,8,576]{0,2,1:T(8,128)(2,1)S(1)}, bf16[128,8,576]{0,2,1:T(8,128)(2,1)}, u32[]{:S(2)}) copy-start(bf16[128,8,576]{0,2,1:T(8,128)(2,1)} %param.5) | copy-start | bytes 3538948
  51.0 3.3 %copy-start.1 = (bf16[128,8,512]{2,1,0:T(8,128)(2,1)S(1)}, bf16[128,8,512]{2,1,0:T(8,128)(2,1)}, u32[]{:S(2)}) copy-start(bf16[128,8,512]{2,1,0:T(8,128)(2,1)} %param.7) | copy-start | bytes 3145732
  63.5 2.5 %copy-start.12 = (bf16[2048,576]{0,1:T(8,128)(2,1)S(1)}, bf16[2048,576]{0,1:T(8,128)(2,1)}, u32[]{:S(2)}) copy-start(bf16[2048,576]{0,1:T(8,128)(2,1)} %all-gather.3.cloned.1.call-done) | copy-start | bytes 7077892
  67.2 1.2 copy-start.3
  68.4 1.2 copy-start.2
  78.2 1.2 copy-start.15
  82.2 1.0 copy-start.6
  87.9 1.9 copy-start.8
  90.9 3.6 %copy-start.10 = (bf16[1024,512]{0,1:T(8,128)(2,1)}, bf16[1024,512]{0,1:T(8,128)(2,1)S(1)}, u32[]{:S(2)}) copy-start(bf16[1024,512]{0,1:T(8,128)(2,1)S(1)} %multiply_convert_fusion.2) | copy-start | bytes 3145732
  95.6 1.0 copy-start.4
  99.8 1.2 copy-start.9
  99.8 2.0 copy-start.13
  101.8 1.2 copy-start.7
  103.1 1.2 copy-start.11
  104.3 1.2 copy-start.5
Sparse Core Ops, SparseCore 0:
  10.3 53.2 all-gather.2
  100.0 81.4 reduce-scatter.1
where the time goes:
time: 227 us; the launch traced here: 226 us
  waiting for transfers between devices  80.1 us (35%)
  blocking collectives  63.5 us (28%)
  matrix products  33 us (15%)
  local copies, waits for them, and re-layouts  32.4 us (14%)
  between operations  14.5 us (6%)
  other arithmetic  2.88 us (1%)
    reduce_scatter x1, waiting for transfers between devices, local(): owned = lax.psum_scatter(dkv, 'ctx', scatter_dimension=0, tiled=True)  71.4 us
    psum x1, blocking collectives, local(): d_latent = lax.psum(owned, 'tp').astype(jnp.bfloat16)  38.1 us
    all_gather x1, blocking collectives, local(): key_pos = lax.all_gather(positions, 'ctx', axis=0, tiled=True)  25.4 us
    dot_general x8, matrix products, contract_first(): lax.dot_general(left, right, (((0,), (0,)), ((), ())), preferred_element_...  13.3 us
    gather x4, local copies, waits for them, and re-layouts, token_mask(): key_docs = doc_ids[key_pos]  12.6 us
    dot_general x8, matrix products, contract_last(): lax.dot_general(left, right, (((1,), (1,)), ((), ())), preferred_element_...  10.4 us
    unnamed x36, local copies, waits for them, and re-layouts  8.64 us
    all_gather x1, waiting for transfers between devices, local(): keys = lax.all_gather(latent, 'ctx', axis=0, tiled=True)  7.95 us
  transfers between devices with their start and end apart: 2, of which 2 were waited for; matrix products, arithmetic and copies ran while one was open for 13% of the time, Pallas kernels for 0%

commit v1 on v0

v1 whole, which is shorter than its diff:
```python
import functools

import jax
import jax.numpy as jnp
from jax import lax
from jax.experimental import pallas as pl
from jax.experimental.pallas import tpu as pltpu
from jax.sharding import PartitionSpec as P

MESH = pl.DeviceIdType.MESH
F32, BF16, I32 = jnp.float32, jnp.bfloat16, jnp.int32
SCALE = 192.0 ** (-0.5)
LOG2E = 1.4426950408889634
WIDTH, LAT, TOK, HEADS, RUN = 576, 512, 128, 8, 64
ROWS = HEADS * RUN
N_CTX, N_TP, N_DOCS = 16, 8, 4
TILES = N_CTX + 1
BLOCKS = 5
PIECE = 80


def dot(left, right):
    return jnp.dot(left, right, preferred_element_type=F32)


def dot_nt(left, right):
    return lax.dot_general(left, right, (((1,), (1,)), ((), ())), preferred_element_type=F32)


def remote(src, dst, send, recv, device):
    return pltpu.make_async_remote_copy(
        src_ref=src, dst_ref=dst, send_sem=send, recv_sem=recv, device_id=device, device_id_type=MESH
    )


def greet(devices):
    barrier = pltpu.get_barrier_semaphore()
    for device in devices:
        pl.semaphore_signal(barrier, inc=1, device_id=device, device_id_type=MESH)
    pl.semaphore_wait(barrier, len(devices))


def gather_kernel(
    latent, positions, docs, query, d_out,
    all_latent, all_positions, starts, q_rows, q_cols, g_rows, g_cols,
    q_in, g_in, g_wide, own_sem, in_sem, send_sem, recv_sem, core_send, core_recv, pos_send, pos_recv,
):
    ctx, tp = lax.axis_index("ctx"), lax.axis_index("tp")
    core, group = lax.rem(ctx, 2), ctx // 2
    twin = (2 * group + 1 - core, tp)
    load_q = pltpu.make_async_copy(query, q_in, in_sem.at[0])
    load_g = pltpu.make_async_copy(d_out, g_in, in_sem.at[1])
    load_q.start()
    load_g.start()
    own = [
        pltpu.make_async_copy(latent, all_latent.at[ctx], own_sem.at[0]),
        pltpu.make_async_copy(positions, all_positions.at[ctx], own_sem.at[1]),
    ]
    for copy in own:
        copy.start()
    same = [(2 * lax.rem(group + k, 8) + core, tp) for k in range(1, 8)]
    every = [(lax.rem(ctx + k, N_CTX), tp) for k in range(1, N_CTX)]
    greet(every)
    sends = []
    for k, device in enumerate(same):
        sends.append(remote(latent, all_latent.at[ctx], send_sem.at[k], recv_sem.at[k], device))
    sends.append(remote(latent, all_latent.at[ctx], core_send.at[7], core_recv.at[7], twin))
    small = []
    for k, device in enumerate(every):
        small.append(remote(positions, all_positions.at[ctx], pos_send.at[k], pos_recv.at[k], device))
    for copy in sends + small:
        copy.start()

    counts = [jnp.sum((docs[...] < value).astype(I32), keepdims=True) for value in range(1, N_DOCS)]
    row = lax.broadcasted_iota(I32, (8, TOK), 0)
    table = jnp.zeros((8, TOK), I32)
    for index, count in enumerate(counts):
        table = jnp.where(row == index, count, table)
    starts[...] = table

    load_q.wait()
    for h in range(HEADS):
        columns = q_in[h]
        rows = columns.T
        for run in range(2):
            q_rows[run, RUN * h : RUN * (h + 1), :] = rows[RUN * run : RUN * (run + 1)]
    for run in range(2):
        for part in range(ROWS // 128):
            pair = slice(128 * part, 128 * (part + 1))
            q_cols[run, :, pair] = q_rows[run, pair, :].T
    load_g.wait()
    for part in range(LAT // 128):
        lanes = slice(128 * part, 128 * (part + 1))
        g_wide[part] = g_in[:, lanes].astype(F32)
        for h in range(HEADS):
            rows = g_wide[part, pl.ds(h, TOK, HEADS), :].astype(BF16)
            for run in range(2):
                g_rows[run, RUN * h : RUN * (h + 1), lanes] = rows[RUN * run : RUN * (run + 1)]
    for run in range(2):
        for part in range(ROWS // 128):
            pair = slice(128 * part, 128 * (part + 1))
            g_cols[run, :, pair] = g_rows[run, pair, :].T

    forwards = []
    for k in range(7):
        slot = 2 * lax.rem(group + 8 - (k + 1), 8) + core
        block = all_latent.at[slot]
        sends[k].wait_send()
        remote(latent, block, send_sem.at[k], recv_sem.at[k], same[k]).wait_recv()
        forward = remote(block, block, core_send.at[k], core_recv.at[k], twin)
        forward.start()
        forwards.append(forward)
    for copy in forwards + sends[7:] + small:
        copy.wait()
    for copy in own:
        copy.wait()


def gather(latent, positions, docs, query, d_out):
    whole, fast = pl.BlockSpec(memory_space=pl.ANY), pl.BlockSpec(memory_space=pltpu.VMEM)
    return pl.pallas_call(
        gather_kernel,
        out_shape=[
            jax.ShapeDtypeStruct((N_CTX, WIDTH, TOK), BF16),
            jax.ShapeDtypeStruct((N_CTX, 1, TOK), I32),
            jax.ShapeDtypeStruct((8, TOK), I32),
            jax.ShapeDtypeStruct((2, ROWS, WIDTH), BF16),
            jax.ShapeDtypeStruct((2, WIDTH, ROWS), BF16),
            jax.ShapeDtypeStruct((2, ROWS, LAT), BF16),
            jax.ShapeDtypeStruct((2, LAT, ROWS), BF16),
        ],
        in_specs=[whole, whole, fast, whole, whole],
        out_specs=[whole, whole] + [fast] * 5,
        scratch_shapes=[
            pltpu.VMEM((HEADS, WIDTH, TOK), BF16),
            pltpu.VMEM((TOK * HEADS, LAT), BF16),
            pltpu.VMEM((LAT // 128, TOK * HEADS, 128), F32),
            pltpu.SemaphoreType.DMA((2,)),
            pltpu.SemaphoreType.DMA((2,)),
            pltpu.SemaphoreType.DMA((7,)),
            pltpu.SemaphoreType.DMA((7,)),
            pltpu.SemaphoreType.DMA((8,)),
            pltpu.SemaphoreType.DMA((8,)),
            pltpu.SemaphoreType.DMA((15,)),
            pltpu.SemaphoreType.DMA((15,)),
        ],
        compiler_params=pltpu.CompilerParams(
            collective_id=0, has_side_effects=True, vmem_limit_bytes=48 << 20
        ),
        name="gather",
    )(latent, positions, docs, query, d_out)


def attention_kernel(
    places, starts, mine, latent, q_rows, q_cols, g_rows, g_cols,
    d_query, partial,
    where_is, keys, score, grad_p, dq, dkv,
):
    for device in range(N_CTX):
        for half in range(2):
            where_is[places[device, 0, RUN * half] // RUN] = 2 * device + half
    low = lax.broadcasted_iota(I32, (WIDTH, TOK), 1) < RUN
    keys[0] = jnp.zeros((WIDTH, TOK), BF16)
    dkv[...] = jnp.zeros_like(dkv)

    def halves(first, second, first_half, second_half):
        first = jnp.where(first_half == 0, first, pltpu.roll(first, RUN, 1))
        second = jnp.where(second_half == 1, second, pltpu.roll(second, RUN, 1))
        return jnp.where(low, first, second)

    def sort(tile, carry):
        one, two = where_is[2 * tile], where_is[2 * tile + 1]
        keys[tile + 1] = halves(
            latent[one // 2].astype(F32), latent[two // 2].astype(F32), one % 2, two % 2
        ).astype(BF16)
        return carry

    lax.fori_loop(0, N_CTX, sort, 0)
    bounds = [starts[index, 0] for index in range(N_DOCS - 1)]

    for run in range(2):
        base = mine[0, RUN * run]
        position = base + lax.broadcasted_iota(I32, (ROWS, 1), 0) % RUN
        begin = jnp.zeros((ROWS, 1), I32)
        oldest = jnp.int32(0)
        for bound in bounds:
            begin = jnp.where(position >= bound, bound, begin)
            oldest = jnp.where(base >= bound, bound, oldest)
        last = base // TOK + 2
        count = (last - 1 - oldest // TOK + 1) // 2

        def block_of(index):
            first = last - 2 * (index + 1)
            return first, jnp.concatenate([keys[first], keys[first + 1]], axis=1)

        def scores(index, peak):
            first, block = block_of(index)
            at = (first - 1) * TOK + lax.broadcasted_iota(I32, (ROWS, 2 * TOK), 1)
            allowed = (at <= position) & (at >= begin)
            value = jnp.where(allowed, dot(q_rows[run], block) * (SCALE * LOG2E), -1e30)
            score[index] = value
            grad_p[index] = dot(g_rows[run], block[:LAT])
            return jnp.maximum(peak, jnp.maximum(value[:, :TOK], value[:, TOK:]))

        peak = lax.fori_loop(0, count, scores, jnp.full((ROWS, TOK), -1e30, F32))
        peak = jnp.max(peak, axis=1, keepdims=True)

        def sums(index, carry):
            total, mixed = carry
            weight = jnp.exp2(score[index] - peak)
            score[index] = weight
            product = weight * grad_p[index]
            return (
                total + weight[:, :TOK] + weight[:, TOK:],
                mixed + product[:, :TOK] + product[:, TOK:],
            )

        zero = jnp.zeros((ROWS, TOK), F32)
        total, mixed = lax.fori_loop(0, count, sums, (zero, zero))
        inverse = 1.0 / jnp.sum(total, axis=1, keepdims=True)
        delta = jnp.sum(mixed, axis=1, keepdims=True) * inverse
        dq[run] = jnp.zeros((ROWS, WIDTH), F32)

        def grads(index, carry):
            first, block = block_of(index)
            prob = score[index] * inverse
            grad_s = (prob * (grad_p[index] - delta) * SCALE).astype(BF16)
            dq[run] += dot_nt(grad_s, block)
            d_keys = dot(q_cols[run], grad_s)
            d_values = dot(g_cols[run], prob.astype(BF16))
            for half in range(2):
                columns = slice(TOK * half, TOK * (half + 1))
                dkv[first + half, :LAT] += d_keys[:LAT, columns] + d_values[:, columns]
                dkv[first + half, LAT:] += d_keys[LAT:, columns]
            return carry

        lax.fori_loop(0, count, grads, 0)

    for h in range(HEADS):
        rows = slice(RUN * h, RUN * (h + 1))
        both = jnp.concatenate([dq[0, rows, :], dq[1, rows, :]], axis=0)
        d_query[h] = both.T.astype(BF16)

    def unsort(device, carry):
        one, two = places[device, 0, 0] // RUN, places[device, 0, RUN] // RUN
        owner = device // 2 + 8 * (device % 2)
        partial[owner] = halves(
            dkv[one // 2 + 1], dkv[two // 2 + 1], one % 2, two % 2
        ).astype(BF16)
        return carry

    lax.fori_loop(0, N_CTX, unsort, 0)


def attention(places, starts, mine, latent, q_rows, q_cols, g_rows, g_cols):
    fast, scalar = pl.BlockSpec(memory_space=pltpu.VMEM), pl.BlockSpec(memory_space=pltpu.SMEM)
    return pl.pallas_call(
        attention_kernel,
        out_shape=[
            jax.ShapeDtypeStruct((HEADS, WIDTH, TOK), BF16),
            jax.ShapeDtypeStruct((N_CTX, WIDTH, TOK), BF16),
        ],
        in_specs=[scalar] * 3 + [fast] * 5,
        out_specs=[fast, fast],
        scratch_shapes=[
            pltpu.SMEM((2 * N_CTX,), I32),
            pltpu.VMEM((TILES, WIDTH, TOK), BF16),
            pltpu.VMEM((BLOCKS, ROWS, 2 * TOK), F32),
            pltpu.VMEM((BLOCKS, ROWS, 2 * TOK), F32),
            pltpu.VMEM((2, ROWS, WIDTH), F32),
            pltpu.VMEM((TILES, WIDTH, TOK), F32),
        ],
        compiler_params=pltpu.CompilerParams(vmem_limit_bytes=56 << 20),
        name="attention",
    )(places, starts, mine, latent, q_rows, q_cols, g_rows, g_cols)


def total_kernel(
    partial, result,
    half, twin_part, chip, group_part, ours, piece_part, piece, final_part,
    in_sem, core_send, core_recv, ctx_send, ctx_recv, tp_send, tp_recv, out_send, out_recv,
):
    ctx, tp = lax.axis_index("ctx"), lax.axis_index("tp")
    core, group = lax.rem(ctx, 2), ctx // 2
    twin = (2 * group + 1 - core, tp)
    same = [(2 * lax.rem(group + k, 8) + core, tp) for k in range(1, 8)]
    heads = [(ctx, lax.rem(tp + k, N_TP)) for k in range(1, N_TP)]

    def rows_of(index):
        return pl.ds(pl.multiple_of(144 * (index // 2) + 64 * lax.rem(index, 2), 16), PIECE)

    load = pltpu.make_async_copy(partial.at[pl.ds(8 * core, 8)], half, in_sem)
    load.start()
    greet([twin] + same + heads)
    to_twin = []
    for k in range(8):
        owner = lax.rem(group + k, 8)
        copy = remote(
            partial.at[8 * (1 - core) + owner], twin_part.at[k], core_send.at[k], core_recv.at[k], twin
        )
        copy.start()
        to_twin.append(copy)
    load.wait()
    to_group = []
    for k in list(range(1, 8)) + [0]:
        owner = lax.rem(group + k, 8)
        to_twin[k].wait_recv()
        both = half[owner].astype(F32) + twin_part[k].astype(F32)
        if k:
            chip[k - 1] = both.astype(BF16)
            copy = remote(
                chip.at[k - 1], group_part.at[k - 1], ctx_send.at[k - 1], ctx_recv.at[k - 1], same[k - 1]
            )
            copy.start()
            to_group.append(copy)
        else:
            mine = both
    for copy in to_group:
        copy.wait_recv()
    for k in range(7):
        mine = mine + group_part[k].astype(F32)
    ours[...] = mine.astype(BF16)
    to_heads = []
    for k in range(7):
        rows = rows_of(lax.rem(tp + k + 1, N_TP))
        copy = remote(ours.at[rows], piece_part.at[k], tp_send.at[k], tp_recv.at[k], heads[k])
        copy.start()
        to_heads.append(copy)
    mine = ours[rows_of(tp), :].astype(F32)
    for copy in to_heads:
        copy.wait_recv()
    for k in range(7):
        mine = mine + piece_part[k].astype(F32)
    piece[...] = mine.astype(BF16)
    to_all = []
    for k in range(7):
        copy = remote(piece, final_part.at[k], out_send.at[k], out_recv.at[k], heads[k])
        copy.start()
        to_all.append(copy)
    result[rows_of(tp), :] = piece[...]
    for k in range(7):
        to_all[k].wait_recv()
        result[rows_of(lax.rem(tp + 7 - k, N_TP)), :] = final_part[k]
    for copy in to_twin + to_group + to_heads + to_all:
        copy.wait_send()


def total(partial):
    dma = pltpu.SemaphoreType.DMA
    return pl.pallas_call(
        total_kernel,
        out_shape=jax.ShapeDtypeStruct((WIDTH, TOK), BF16),
        in_specs=[pl.BlockSpec(memory_space=pl.ANY)],
        out_specs=pl.BlockSpec(memory_space=pltpu.VMEM),
        scratch_shapes=[
            pltpu.VMEM((8, WIDTH, TOK), BF16),
            pltpu.VMEM((8, WIDTH, TOK), BF16),
            pltpu.VMEM((7, WIDTH, TOK), BF16),
            pltpu.VMEM((7, WIDTH, TOK), BF16),
            pltpu.VMEM((WIDTH, TOK), BF16),
            pltpu.VMEM((7, PIECE, TOK), BF16),
            pltpu.VMEM((PIECE, TOK), BF16),
            pltpu.VMEM((7, PIECE, TOK), BF16),
            dma,
            dma((8,)),
            dma((8,)),
            dma((7,)),
            dma((7,)),
            dma((7,)),
            dma((7,)),
            dma((7,)),
            dma((7,)),
        ],
        compiler_params=pltpu.CompilerParams(
            collective_id=1, has_side_effects=True, vmem_limit_bytes=48 << 20
        ),
        name="total",
    )(partial)


def local(query, latent, d_out, positions, doc_ids):
    here = positions.reshape(1, TOK)
    columns, places, starts, q_rows, q_cols, g_rows, g_cols = gather(
        latent.T,
        here,
        doc_ids.reshape(-1, TOK),
        query.transpose(1, 2, 0),
        d_out.reshape(TOK * HEADS, LAT),
    )
    d_query, partial = attention(places, starts, here, columns, q_rows, q_cols, g_rows, g_cols)
    d_latent = total(partial)
    return (d_query.transpose(2, 0, 1), d_latent.T)


def solution(mesh):
    return jax.shard_map(
        local,
        mesh=mesh,
        in_specs=(P("ctx", "tp", None), P("ctx", None), P("ctx", "tp", None), P("ctx"), P()),
        out_specs=(P("ctx", "tp", None), P("ctx", None)),
        check_vma=False,
    )
```

time: 227 us -> 95.4 us (0.42)
  Pallas kernels: 0 us -> 82.6 us
  waiting for transfers between devices: 80.1 us -> 0 us
  blocking collectives: 63.5 us -> 0 us
  matrix products: 33 us -> 0 us
  local copies, waits for them, and re-layouts: 32.4 us -> 11.3 us
  between operations: 14.5 us -> 0.67 us
  other arithmetic: 2.88 us -> 0 us
    pallas_call x0 -> x3, Pallas kernels: none -> 82.6 us  [the longest x1 37.8 us: total(): pl.pallas_call(total_kernel, out_shape=jax.ShapeDtypeStruct((WIDTH, TOK),...]
    reduce_scatter x1 -> x0, waiting for transfers between devices: 71.4 us -> none  [local(): owned = lax.psum_scatter(dkv, 'ctx', scatter_dimension=0, tiled=True)]
    psum x1 -> x0, blocking collectives: 38.1 us -> none  [local(): d_latent = lax.psum(owned, 'tp').astype(jnp.bfloat16)]
    dot_general x24 -> x0, matrix products: 33 us -> none  [the longest x8 13.3 us: contract_first(): lax.dot_general(left, right, (((0,), (0,)), ((), ())), preferred_element_...]
    all_gather x1 -> x0, blocking collectives: 25.4 us -> none  [local(): key_pos = lax.all_gather(positions, 'ctx', axis=0, tiled=True)]
    gather x5 -> x0, local copies, waits for them, and re-layouts: 13.7 us -> none  [the longest x4 12.6 us: token_mask(): key_docs = doc_ids[key_pos]]
    all_gather x1 -> x0, waiting for transfers between devices: 7.95 us -> none  [local(): keys = lax.all_gather(latent, 'ctx', axis=0, tiled=True)]
    reshape x7 -> x0, local copies, waits for them, and re-layouts: 6.62 us -> none  [the longest x6 5.31 us: row_mask(): jnp.broadcast_to(mask[:, None, :], (tok, heads, mask.shape[1]))]
  transfers between devices with their start and end apart: 2 -> 0, of which waited for: 2 -> 0; matrix products, arithmetic and copies ran while one was open for 13% -> 0% of each run, Pallas kernels for 0% -> 0%
where the time goes in v1:
time: 95.4 us; the launch traced here: 94.6 us
  Pallas kernels  82.6 us (87%)
  local copies, waits for them, and re-layouts  11.3 us (12%)
    pallas_call x1, Pallas kernels, total(): pl.pallas_call(total_kernel, out_shape=jax.ShapeDtypeStruct((WIDTH, TOK),...  37.8 us
    pallas_call x1, Pallas kernels, gather(): pl.pallas_call(gather_kernel, out_shape=[jax.ShapeDtypeStruct((N_CTX, WID...  26 us
    pallas_call x1, Pallas kernels, attention(): pl.pallas_call(attention_kernel, out_shape=[jax.ShapeDtypeStruct((HEADS,...  18.8 us
    unnamed x23, local copies, waits for them, and re-layouts  11.3 us

profile of v1, /device:TPU:0, one launch (start us, length us, event | category | flops | bytes accessed | tf_op | source)
XLA Modules:
  0.0 94.6 jit_solution(7738512733503127200)
XLA Ops:
  0.6 0.0 copy-start.2
  0.6 1.3 %copy-done.2 = bf16[128,8,576]{0,2,1:T(8,128)(2,1)S(1)} copy-done((bf16[128,8,576]{0,2,1:T(8,128)(2,1)S(1)}, bf16[128,8,576]{0,2,1:T(8,128)(2,1)}, u32[]{:S(2)}) %copy-start.2) | copy-done | bytes 1179672
  1.9 0.0 copy-start.5
  1.9 1.2 %copy-done.5 = bf16[128,8,512]{2,1,0:T(8,128)(2,1)S(1)} copy-done((bf16[128,8,512]{2,1,0:T(8,128)(2,1)S(1)}, bf16[128,8,512]{2,1,0:T(8,128)(2,1)}, u32[]{:S(2)}) %copy-start.5) | copy-done | bytes 1048600
  3.1 0.0 copy-start.6
  3.1 0.9 copy-done.6
  4.0 0.7 copy-done.7
  4.7 0.0 copy-start.10
  4.7 0.7 copy-done.10
  5.4 26.0 %gather.1 = (bf16[16,576,128]{2,1,0:T(8,128)(2,1)}, s32[16,1,128]{2,1,0:T(1,128)S(1)}, s32[8,128]{1,0:T(8,128)S(1)}, bf16[2,512,576]{2,1,0:T(8,128)(2,1)}, bf16[...) custom-call(bf16[576,128]{1,0:T(8,128)(2,1)S(1)} %bitcast.10, ...), custom_call_target="tpu_custom_call" | custom-call | tf_op jit(solution)/shard_map/gather/pallas_call | solution.py:121
  31.4 0.0 copy-start.1
  31.4 1.0 %copy-done.1 = bf16[2,576,512]{2,1,0:T(8,128)(2,1)} copy-done((bf16[2,576,512]{2,1,0:T(8,128)(2,1)}, bf16[2,576,512]{2,1,0:T(8,128)(2,1)S(1)}, u32[]{:S(2)}) %copy-start.1) | copy-done | bytes 1179672
  32.4 0.0 copy-start.3
  32.4 1.0 %copy-done.3 = bf16[2,512,512]{2,1,0:T(8,128)(2,1)} copy-done((bf16[2,512,512]{2,1,0:T(8,128)(2,1)}, bf16[2,512,512]{2,1,0:T(8,128)(2,1)S(1)}, u32[]{:S(2)}) %copy-start.3) | copy-done | bytes 1048600
  33.4 0.0 copy-start.4
  33.4 1.0 %copy-done.4 = bf16[2,512,512]{2,1,0:T(8,128)(2,1)} copy-done((bf16[2,512,512]{2,1,0:T(8,128)(2,1)}, bf16[2,512,512]{2,1,0:T(8,128)(2,1)S(1)}, u32[]{:S(2)}) %copy-start.4) | copy-done | bytes 1048600
  34.5 0.0 copy-start.8
  34.5 0.6 copy-done.8
  35.1 0.0 copy-start.9
  35.1 0.6 copy-done.9
  35.7 18.8 %attention.1 = (bf16[8,576,128]{2,1,0:T(8,128)(2,1)}, bf16[16,576,128]{2,1,0:T(8,128)(2,1)}) custom-call(s32[16,1,128]{2,1,0:T(1,128)} %copy-done.8, s32[8,128]{1,0:T(8,128)} %copy-done.9, s32[1,128]{1,0:T(1,128)} %bitcast.12, bf16[16,576,128]{2,1,0:T(8,128)(2,1)} %get-tuple-element.13.latent, bf16[2,512,576]{2,1,0:T(8,128)(2,1)} %get-tuple-element.14.q_rows, ...), custom_call_target="tpu_custom_call" | custom-call | tf_op jit(solution)/shard_map/attention/pallas_call | solution.py:257
  54.5 1.7 %copy-done = bf16[16,576,128]{2,1,0:T(8,128)(2,1)S(1)} copy-done((bf16[16,576,128]{2,1,0:T(8,128)(2,1)S(1)}, bf16[16,576,128]{2,1,0:T(8,128)(2,1)}, u32[]{:S(2)}) %copy-start) | copy-done | bytes 2359320
  56.1 37.8 %total.1 = bf16[576,128]{1,0:T(8,128)(2,1)S(1)} custom-call(bf16[16,576,128]{2,1,0:T(8,128)(2,1)S(1)} %copy-done), custom_call_target="tpu_custom_call" | custom-call | tf_op jit(solution)/shard_map/total/pallas_call | solution.py:350
  93.9 0.7 copy.8
  (2 shorter events, 0.0 us)
Async XLA Ops:
  0.6 1.3 %copy-start.2 = (bf16[128,8,576]{0,2,1:T(8,128)(2,1)S(1)}, bf16[128,8,576]{0,2,1:T(8,128)(2,1)}, u32[]{:S(2)}) copy-start(bf16[128,8,576]{0,2,1:T(8,128)(2,1)} %param.5) | copy-start | bytes 3538948
  1.9 1.2 %copy-start.5 = (bf16[128,8,512]{2,1,0:T(8,128)(2,1)S(1)}, bf16[128,8,512]{2,1,0:T(8,128)(2,1)}, u32[]{:S(2)}) copy-start(bf16[128,8,512]{2,1,0:T(8,128)(2,1)} %param.7) | copy-start | bytes 3145732
  3.1 0.9 copy-start.6
  4.0 0.7 copy-start.7
  4.7 0.7 copy-start.10
  31.4 1.0 %copy-start.1 = (bf16[2,576,512]{2,1,0:T(8,128)(2,1)}, bf16[2,576,512]{2,1,0:T(8,128)(2,1)S(1)}, u32[]{:S(2)}) copy-start(bf16[2,576,512]{2,1,0:T(8,128)(2,1)S(1)} %get-tuple-element.15.q_cols) | copy-start | bytes 3538948
  32.4 1.0 %copy-start.3 = (bf16[2,512,512]{2,1,0:T(8,128)(2,1)}, bf16[2,512,512]{2,1,0:T(8,128)(2,1)S(1)}, u32[]{:S(2)}) copy-start(bf16[2,512,512]{2,1,0:T(8,128)(2,1)S(1)} %get-tuple-element.16.g_rows) | copy-start | bytes 3145732
  33.4 1.0 %copy-start.4 = (bf16[2,512,512]{2,1,0:T(8,128)(2,1)}, bf16[2,512,512]{2,1,0:T(8,128)(2,1)S(1)}, u32[]{:S(2)}) copy-start(bf16[2,512,512]{2,1,0:T(8,128)(2,1)S(1)} %get-tuple-element.17.g_cols) | copy-start | bytes 3145732
  34.5 0.6 copy-start.8
  35.1 0.6 copy-start.9
  54.5 1.7 %copy-start = (bf16[16,576,128]{2,1,0:T(8,128)(2,1)S(1)}, bf16[16,576,128]{2,1,0:T(8,128)(2,1)}, u32[]{:S(2)}) copy-start(bf16[16,576,128]{2,1,0:T(8,128)(2,1)} %get-tuple-element.19.partial) | copy-start | bytes 7077892

commit v2 on v0

v2 whole, which is shorter than its diff:
```python
import jax
import jax.numpy as jnp
from jax import lax
from jax.experimental import pallas as pl
from jax.experimental.pallas import tpu as pltpu
from jax.sharding import PartitionSpec as P

MESH = pl.DeviceIdType.MESH
F32, BF16, I32 = jnp.float32, jnp.bfloat16, jnp.int32
SCALE = 192.0 ** (-0.5)
LOG2E = 1.4426950408889634
WIDTH, LAT, TOK, HEADS, RUN = 576, 512, 128, 8, 64
ROWS = HEADS * RUN
N_CTX, N_TP, N_DOCS = 16, 8, 4
SLOTS = 9
SPAN = SLOTS * TOK
QUARTER = WIDTH // 4
X_PIECE, Y_PIECE = 80, 64
X_ROWS, Y_ROWS = 4 * X_PIECE, 4 * Y_PIECE
INVERSE, STARTS = N_CTX, N_CTX + 1


def dot(left, right):
    return jnp.dot(left, right, preferred_element_type=F32)


def dot_nt(left, right):
    return lax.dot_general(left, right, (((1,), (1,)), ((), ())), preferred_element_type=F32)


def remote(src, dst, send, recv, device):
    return pltpu.make_async_remote_copy(
        src_ref=src, dst_ref=dst, send_sem=send, recv_sem=recv, device_id=device, device_id_type=MESH
    )


def greet(devices):
    barrier = pltpu.get_barrier_semaphore()
    for device in devices:
        pl.semaphore_signal(barrier, inc=1, device_id=device, device_id_type=MESH)
    pl.semaphore_wait(barrier, len(devices))


def kernel(
    latent, positions, docs, query, d_out, d_query, d_latent,
    q_in, g_in, g_wide, q_rows, q_cols, g_rows, g_cols, blocks, places, info, table,
    keys, score, grad_p, prob, grad_s, dkv, dq,
    x_part, y_part, x_twin, y_twin, x_chip, y_chip, x_recv, y_recv, x_sum, y_sum,
    x_last, y_last, piece, pieces,
    in_sem, info_sem, a_send, a_recv, b_send, b_recv, c_send, c_recv, pos_send, pos_recv,
    t_send, t_recv, x_send, x_got, y_send, y_got, xl_send, xl_got, yl_send, yl_got, o_send, o_recv,
):
    ctx, tp = lax.axis_index("ctx"), lax.axis_index("tp")
    core, group = lax.rem(ctx, 2), ctx // 2
    x, low_z = tp // 2, lax.rem(tp, 2)

    def turn(index, step, size):
        return lax.rem(index + step + size, size)

    def along_x(step):
        return (ctx, 2 * turn(x, step, 4) + low_z)

    twin = (2 * group + 1 - core, tp)
    same = [(2 * turn(group, k, 8) + core, tp) for k in range(1, 8)]
    every = [(turn(ctx, k, N_CTX), tp) for k in range(1, N_CTX)]
    over_tp = [(ctx, turn(tp, k, N_TP)) for k in range(1, N_TP)]
    plane = [
        (2 * turn(group, k, 8) + core, 2 * x + turn(low_z, j, 2))
        for j in range(2) for k in range(8) if j or k
    ]

    loads = [
        pltpu.make_async_copy(latent, blocks.at[ctx], in_sem.at[0]),
        pltpu.make_async_copy(query, q_in, in_sem.at[1]),
        pltpu.make_async_copy(d_out, g_in, in_sem.at[2]),
    ]
    for copy in loads:
        copy.start()
    places[ctx] = positions[...]
    greet(every + over_tp + plane[7:][1:])

    def quarter(index):
        return pl.ds(pl.multiple_of(QUARTER * index, 16), QUARTER)

    small = []
    for k, device in enumerate(every):
        mine = places.at[ctx]
        small.append(remote(mine, mine, pos_send.at[k], pos_recv.at[k], device))
    for copy in small:
        copy.start()
    loads[0].wait()
    first = []
    for k, device in enumerate(same):
        for j in range(2):
            part = blocks.at[ctx, quarter(turn(x, j, 4))]
            copy = remote(part, part, a_send.at[2 * k + j], a_recv.at[2 * k + j], device)
            copy.start()
            first.append(copy)
    to_twin = [remote(blocks.at[ctx], blocks.at[ctx], c_send.at[7], c_recv.at[7], twin)]
    to_twin[0].start()

    loads[1].wait()
    for h in range(HEADS):
        rows = q_in[h].T
        for run in range(2):
            q_rows[run, RUN * h : RUN * (h + 1), :] = rows[RUN * run : RUN * (run + 1)]

    def sender(k):
        return 2 * turn(group, -(k + 1), 8) + core

    second = []
    for k in range(7):
        for j in range(2):
            part = blocks.at[sender(k), quarter(turn(x, j, 4))]
            at = 2 * k + j
            remote(part, part, a_send.at[at], a_recv.at[at], same[k]).wait_recv()
            copy = remote(part, part, b_send.at[at], b_recv.at[at], along_x(1 - 2 * j))
            copy.start()
            second.append(copy)

    for run in range(2):
        for part in range(ROWS // 128):
            pair = slice(128 * part, 128 * (part + 1))
            q_cols[run, :, pair] = q_rows[run, pair, :].T
    loads[2].wait()
    for part in range(LAT // 128):
        lanes = slice(128 * part, 128 * (part + 1))
        g_wide[part] = g_in[:, lanes].astype(F32)
        for h in range(HEADS):
            rows = g_wide[part, pl.ds(h, TOK, HEADS), :].astype(BF16)
            for run in range(2):
                g_rows[run, RUN * h : RUN * (h + 1), lanes] = rows[RUN * run : RUN * (run + 1)]
    for run in range(2):
        for part in range(ROWS // 128):
            pair = slice(128 * part, 128 * (part + 1))
            g_cols[run, :, pair] = g_rows[run, pair, :].T

    for copy in small:
        copy.wait()
    lane = lax.broadcasted_iota(I32, (N_CTX, TOK), 1)
    device = lax.broadcasted_iota(I32, (N_CTX, TOK), 0)
    at = jnp.concatenate([places[d] for d in range(N_CTX)], axis=0)
    holder = jnp.where(at[:, :1] // RUN == lane, 2 * device, 0)
    holder = holder + jnp.where(at[:, RUN : RUN + 1] // RUN == lane, 2 * device + 1, 0)
    info[:N_CTX] = at
    info[INVERSE : INVERSE + 1] = jnp.sum(holder, axis=0, keepdims=True)
    for value in range(1, N_DOCS):
        count = jnp.sum((docs[...] < value).astype(I32), keepdims=True)
        info[STARTS + value - 1 : STARTS + value] = jnp.broadcast_to(count, (1, TOK))
    copy = pltpu.make_async_copy(info, table, info_sem)
    copy.start()
    copy.wait()

    for k in range(7):
        block = blocks.at[sender(k)]
        for j in range(2):
            part = blocks.at[sender(k), quarter(turn(x, 3 - j, 4))]
            at = 2 * k + j
            remote(part, part, b_send.at[at], b_recv.at[at], along_x(1 - 2 * j)).wait_recv()
        copy = remote(block, block, c_send.at[k], c_recv.at[k], twin)
        copy.start()
        to_twin.append(copy)
    for copy in first + second + to_twin:
        copy.wait_send()
    for k in range(8):
        block = blocks.at[turn(sender(k), 1 - 2 * core, N_CTX)]
        remote(block, block, c_send.at[k], c_recv.at[k], twin).wait_recv()

    bounds = [table[STARTS + index, 0] for index in range(N_DOCS - 1)]
    low = lax.broadcasted_iota(I32, (WIDTH, TOK), 1) < RUN
    bases = [table[ctx, RUN * run] for run in range(2)]
    tops = [base // TOK - (SLOTS - 1) for base in bases]

    for run in range(2):
        for slot in range(SLOTS):
            tile = jnp.clip(tops[run] + slot, 0, N_CTX - 1)
            one, two = (jnp.clip(table[INVERSE, 2 * tile + i], 0, 2 * N_CTX - 1) for i in range(2))
            left, right = blocks[one // 2].astype(F32), blocks[two // 2].astype(F32)
            left = jnp.where(one % 2 == 0, left, pltpu.roll(left, RUN, 1))
            right = jnp.where(two % 2 == 1, right, pltpu.roll(right, RUN, 1))
            keys[run, :, TOK * slot : TOK * (slot + 1)] = jnp.where(low, left, right).astype(BF16)

        position = bases[run] + lax.broadcasted_iota(I32, (ROWS, 1), 0) % RUN
        begin = jnp.zeros((ROWS, 1), I32)
        for bound in bounds:
            begin = jnp.where(position >= bound, bound, begin)
        begin = begin - tops[run] * TOK
        position = position - tops[run] * TOK

        peak = jnp.full((ROWS, TOK), -1e30, F32)
        for start in range(0, SPAN, 2 * TOK):
            size = min(2 * TOK, SPAN - start)
            columns = slice(start, start + size)
            key = start + lax.broadcasted_iota(I32, (ROWS, size), 1)
            allowed = key >= begin
            if start + size == SPAN:
                allowed = allowed & (key <= position)
            value = jnp.where(allowed, dot(q_rows[run], keys[run, :, columns]), -1e30)
            score[:, columns] = value
            grad_p[:, columns] = dot(g_rows[run], keys[run, :LAT, columns])
            for part in range(size // TOK):
                peak = jnp.maximum(peak, value[:, TOK * part : TOK * (part + 1)])
        peak = jnp.max(peak, axis=1, keepdims=True) * (SCALE * LOG2E)

        sums = jnp.zeros((ROWS, TOK), F32)
        mixed = jnp.zeros((ROWS, TOK), F32)
        for slot in range(SLOTS):
            columns = slice(TOK * slot, TOK * (slot + 1))
            weight = jnp.exp2(score[:, columns] * (SCALE * LOG2E) - peak)
            score[:, columns] = weight
            sums = sums + weight
            mixed = mixed + weight * grad_p[:, columns]
        inverse = 1.0 / jnp.sum(sums, axis=1, keepdims=True)
        delta = jnp.sum(mixed, axis=1, keepdims=True) * inverse
        scaled = inverse * SCALE
        for slot in range(SLOTS):
            columns = slice(TOK * slot, TOK * (slot + 1))
            weight = score[:, columns]
            prob[run, :, columns] = (weight * inverse).astype(BF16)
            grad_s[run, :, columns] = (weight * scaled * (grad_p[:, columns] - delta)).astype(BF16)

    def gradient(rows, target):
        size = rows.stop - rows.start
        values = slice(rows.start, min(rows.stop, LAT))
        for run in range(2):
            for start in range(0, SPAN, 2 * TOK):
                width = min(2 * TOK, SPAN - start)
                columns = slice(start, start + width)
                both = dot(q_cols[run, rows, :], grad_s[run, :, columns])
                value = dot(g_cols[run, values, :], prob[run, :, columns])
                if values.stop < rows.stop:
                    value = jnp.concatenate(
                        [value, jnp.zeros((rows.stop - values.stop, width), F32)], axis=0
                    )
                both = both + value
                for part in range(width // TOK):
                    dkv[run, start // TOK + part, :size] = both[:, TOK * part : TOK * (part + 1)]
        first_lanes = lax.broadcasted_iota(I32, (size, TOK), 1) < RUN
        for device in range(N_CTX):
            out = []
            for half in range(2):
                place = table[device, RUN * half] // RUN
                found = jnp.zeros((size, TOK), F32)
                for run in range(2):
                    slot = place // 2 - tops[run]
                    inside = (slot >= 0) & (slot < SLOTS)
                    term = dkv[run, jnp.clip(slot, 0, SLOTS - 1), :size]
                    found = found + jnp.where(inside, term, 0.0)
                out.append(jnp.where(place % 2 == half, found, pltpu.roll(found, RUN, 1)))
            target[device % 2, device // 2] = jnp.where(first_lanes, out[0], out[1]).astype(BF16)

    def query_gradient(run):
        dq[run] = dot_nt(grad_s[run], keys[run])

    gradient(slice(0, X_ROWS), x_part)
    x_swap = remote(x_part.at[1 - core], x_twin, t_send.at[0], t_recv.at[0], twin)
    x_swap.start()
    gradient(slice(X_ROWS, WIDTH), y_part)
    y_swap = remote(y_part.at[1 - core], y_twin, t_send.at[1], t_recv.at[1], twin)
    y_swap.start()

    def x_rows(index):
        return pl.ds(pl.multiple_of(X_PIECE * index, 16), X_PIECE)

    def y_rows(index):
        return pl.ds(pl.multiple_of(Y_PIECE * index, 16), Y_PIECE)

    x_swap.wait_recv()
    for g in range(8):
        x_chip[g] = (x_part[core, g].astype(F32) + x_twin[g].astype(F32)).astype(BF16)
    x_step = []
    for k in range(3):
        source = x_chip.at[:, x_rows(turn(x, k + 1, 4))]
        copy = remote(source, x_recv.at[k], x_send.at[k], x_got.at[k], along_x(k + 1))
        copy.start()
        x_step.append(copy)
    y_swap.wait_recv()
    for g in range(8):
        y_chip[g] = (y_part[core, g].astype(F32) + y_twin[g].astype(F32)).astype(BF16)
    y_step = []
    for k in range(7):
        source = y_chip.at[turn(group, k + 1, 8)]
        copy = remote(source, y_recv.at[k], y_send.at[k], y_got.at[k], same[k])
        copy.start()
        y_step.append(copy)

    for run in range(2):
        query_gradient(run)
    for h in range(HEADS):
        rows = slice(RUN * h, RUN * (h + 1))
        both = jnp.concatenate([dq[0, rows, :], dq[1, rows, :]], axis=0)
        d_query[h] = both.T.astype(BF16)

    for copy in x_step:
        copy.wait_recv()
    for g in range(8):
        total = x_chip[g, x_rows(x), :].astype(F32)
        for k in range(3):
            total = total + x_recv[k, g].astype(F32)
        x_sum[g] = total.astype(BF16)
    x_end = []
    for k, device in enumerate(plane):
        copy = remote(
            x_sum.at[turn(group, (k + 1) % 8, 8)], x_last.at[k], xl_send.at[k], xl_got.at[k], device
        )
        copy.start()
        x_end.append(copy)
    for copy in y_step:
        copy.wait_recv()
    total = y_chip[group].astype(F32)
    for k in range(7):
        total = total + y_recv[k].astype(F32)
    y_sum[...] = total.astype(BF16)
    y_end = []
    for k, device in enumerate(over_tp):
        source = y_sum.at[y_rows(turn(tp, k + 1, N_TP) // 2)]
        copy = remote(source, y_last.at[k], yl_send.at[k], yl_got.at[k], device)
        copy.start()
        y_end.append(copy)

    for copy in x_end:
        copy.wait_recv()
    total = x_sum[group].astype(F32)
    for k in range(15):
        total = total + x_last[k].astype(F32)
    piece[:X_PIECE] = total.astype(BF16)
    for copy in y_end:
        copy.wait_recv()
    total = y_sum[y_rows(x), :].astype(F32)
    for k in range(7):
        total = total + y_last[k].astype(F32)
    piece[X_PIECE:] = total.astype(BF16)
    out_step = []
    for k in range(3):
        copy = remote(piece, pieces.at[k], o_send.at[k], o_recv.at[k], along_x(k + 1))
        copy.start()
        out_step.append(copy)

    def place(index, value):
        d_latent[x_rows(index), :] = value[:X_PIECE]
        d_latent[pl.ds(pl.multiple_of(X_ROWS + Y_PIECE * index, 16), Y_PIECE), :] = value[X_PIECE:]

    place(x, piece[...])
    for k in range(3):
        out_step[k].wait_recv()
        place(turn(x, -(k + 1), 4), pieces[k])
    for copy in [x_swap, y_swap] + x_step + y_step + x_end + y_end + out_step:
        copy.wait_send()


def local(query, latent, d_out, positions, doc_ids):
    whole, fast = pl.BlockSpec(memory_space=pl.ANY), pl.BlockSpec(memory_space=pltpu.VMEM)
    vmem, dma = pltpu.VMEM, pltpu.SemaphoreType.DMA
    d_query, d_latent = pl.pallas_call(
        kernel,
        out_shape=[
            jax.ShapeDtypeStruct((HEADS, WIDTH, TOK), BF16),
            jax.ShapeDtypeStruct((WIDTH, TOK), BF16),
        ],
        in_specs=[whole, fast, fast, whole, whole],
        out_specs=[fast, fast],
        scratch_shapes=[
            vmem((HEADS, WIDTH, TOK), BF16),
            vmem((TOK * HEADS, LAT), BF16),
            vmem((LAT // 128, TOK * HEADS, 128), F32),
            vmem((2, ROWS, WIDTH), BF16),
            vmem((2, WIDTH, ROWS), BF16),
            vmem((2, ROWS, LAT), BF16),
            vmem((2, LAT, ROWS), BF16),
            vmem((N_CTX, WIDTH, TOK), BF16),
            vmem((N_CTX, 1, TOK), I32),
            vmem((24, TOK), I32),
            pltpu.SMEM((24, TOK), I32),
            vmem((2, WIDTH, SPAN), BF16),
            vmem((ROWS, SPAN), F32),
            vmem((ROWS, SPAN), F32),
            vmem((2, ROWS, SPAN), BF16),
            vmem((2, ROWS, SPAN), BF16),
            vmem((2, SLOTS, X_ROWS, TOK), F32),
            vmem((2, ROWS, WIDTH), F32),
            vmem((2, 8, X_ROWS, TOK), BF16),
            vmem((2, 8, Y_ROWS, TOK), BF16),
            vmem((8, X_ROWS, TOK), BF16),
            vmem((8, Y_ROWS, TOK), BF16),
            vmem((8, X_ROWS, TOK), BF16),
            vmem((8, Y_ROWS, TOK), BF16),
            vmem((3, 8, X_PIECE, TOK), BF16),
            vmem((7, Y_ROWS, TOK), BF16),
            vmem((8, X_PIECE, TOK), BF16),
            vmem((Y_ROWS, TOK), BF16),
            vmem((15, X_PIECE, TOK), BF16),
            vmem((7, Y_PIECE, TOK), BF16),
            vmem((X_PIECE + Y_PIECE, TOK), BF16),
            vmem((3, X_PIECE + Y_PIECE, TOK), BF16),
            dma((3,)),
            dma,
        ]
        + [dma((size,)) for size in (14, 14, 8, 15, 2, 3, 7, 15, 7, 3) for _ in range(2)],
        compiler_params=pltpu.CompilerParams(
            collective_id=0, has_side_effects=True, vmem_limit_bytes=63 << 20
        ),
        name="latent_attention_backward",
    )(
        latent.T,
        positions.reshape(1, TOK),
        doc_ids.reshape(-1, TOK),
        query.transpose(1, 2, 0),
        d_out.reshape(TOK * HEADS, LAT),
    )
    return (d_query.transpose(2, 0, 1), d_latent.T)


def solution(mesh):
    return jax.shard_map(
        local,
        mesh=mesh,
        in_specs=(P("ctx", "tp", None), P("ctx", None), P("ctx", "tp", None), P("ctx"), P()),
        out_specs=(P("ctx", "tp", None), P("ctx", None)),
        check_vma=False,
    )
```

time: 227 us -> 64.2 us (0.28)
  waiting for transfers between devices: 80.1 us -> 0 us
  blocking collectives: 63.5 us -> 0 us
  Pallas kernels: 0 us -> 60.3 us
  matrix products: 33 us -> 0 us
  local copies, waits for them, and re-layouts: 32.4 us -> 3.07 us
  between operations: 14.5 us -> 0.65 us
  other arithmetic: 2.88 us -> 0 us
    reduce_scatter x1 -> x0, waiting for transfers between devices: 71.4 us -> none  [local(): owned = lax.psum_scatter(dkv, 'ctx', scatter_dimension=0, tiled=True)]
    pallas_call x0 -> x1, Pallas kernels: none -> 60.3 us  [local(): pl.pallas_call(kernel, out_shape=[jax.ShapeDtypeStruct((HEADS, WIDTH, TOK...]
    psum x1 -> x0, blocking collectives: 38.1 us -> none  [local(): d_latent = lax.psum(owned, 'tp').astype(jnp.bfloat16)]
    dot_general x24 -> x0, matrix products: 33 us -> none  [the longest x8 13.3 us: contract_first(): lax.dot_general(left, right, (((0,), (0,)), ((), ())), preferred_element_...]
    all_gather x1 -> x0, blocking collectives: 25.4 us -> none  [local(): key_pos = lax.all_gather(positions, 'ctx', axis=0, tiled=True)]
    gather x5 -> x0, local copies, waits for them, and re-layouts: 13.7 us -> none  [the longest x4 12.6 us: token_mask(): key_docs = doc_ids[key_pos]]
    all_gather x1 -> x0, waiting for transfers between devices: 7.95 us -> none  [local(): keys = lax.all_gather(latent, 'ctx', axis=0, tiled=True)]
    reshape x7 -> x0, local copies, waits for them, and re-layouts: 6.62 us -> none  [the longest x6 5.31 us: row_mask(): jnp.broadcast_to(mask[:, None, :], (tok, heads, mask.shape[1]))]
  transfers between devices with their start and end apart: 2 -> 0, of which waited for: 2 -> 0; matrix products, arithmetic and copies ran while one was open for 13% -> 0% of each run, Pallas kernels for 0% -> 0%
where the time goes in v2:
time: 64.2 us; the launch traced here: 64 us
  Pallas kernels  60.3 us (94%)
  local copies, waits for them, and re-layouts  3.07 us (5%)
  between operations  0.65 us (1%)
    pallas_call x1, Pallas kernels, local(): pl.pallas_call(kernel, out_shape=[jax.ShapeDtypeStruct((HEADS, WIDTH, TOK...  60.3 us
    unnamed x4, local copies, waits for them, and re-layouts  3.07 us

profile of v2, /device:TPU:0, one launch (start us, length us, event | category | flops | bytes accessed | tf_op | source)
XLA Modules:
  0.0 64.0 jit_solution(14636598877109069683)
XLA Ops:
  0.6 60.3 %latent_attention_backward.1 = (bf16[8,576,128]{2,1,0:T(8,128)(2,1)}, bf16[576,128]{1,0:T(8,128)(2,1)}) custom-call(bf16[576,128]{1,0:T(8,128)(2,1)} %bitcast.11, s32[1,128]{1,0:T(1,128)} %bitcast.13, s32[16,128]{1,0:T(8,128)} %bitcast.12, bf16[8,576,128]{2,1,0:T(8,128)(2,1)} %bitcast.8, bf16[1024,512]{1,0:T(8,128)(2,1)} %bitcast.9), custom_call_target="tpu_custom_call" | custom-call | tf_op jit(solution)/shard_map/latent_attention_backward/pallas_call | solution.py:354
  60.9 0.0 copy-start
  61.0 2.4 %copy.9 = bf16[128,8,576]{0,2,1:T(8,128)(2,1)} copy(bf16[128,8,576]{0,2,1:T(8,128)(2,1)} %bitcast.7) | data formatting | bytes 2359296
  63.4 0.0 copy-done
  63.4 0.7 %copy.10 = bf16[128,576]{0,1:T(8,128)(2,1)} copy(bf16[128,576]{0,1:T(8,128)(2,1)S(1)} %bitcast.10) | data formatting | bytes 294912
Async XLA Ops:
  60.9 2.4 %copy-start = (bf16[576,128]{1,0:T(8,128)(2,1)S(1)}, bf16[576,128]{1,0:T(8,128)(2,1)}, u32[]{:S(2)}) copy-start(bf16[576,128]{1,0:T(8,128)(2,1)} %get-tuple-element.5) | copy-start | bytes 442372

commit v3 on v2

v3 whole, which is shorter than its diff:
```python
import jax
import jax.numpy as jnp
from jax import lax
from jax.experimental import pallas as pl
from jax.experimental.pallas import tpu as pltpu
from jax.sharding import PartitionSpec as P

MESH = pl.DeviceIdType.MESH
F32, BF16, I32 = jnp.float32, jnp.bfloat16, jnp.int32
SCALE = 192.0 ** (-0.5)
LOG2E = 1.4426950408889634
WIDTH, LAT, TOK, HEADS, RUN = 576, 512, 128, 8, 64
ROWS = HEADS * RUN
N_CTX, N_TP, N_DOCS = 16, 8, 4
SLOTS = 9
SPAN = SLOTS * TOK
QUARTER = WIDTH // 4
X_SIZES, Y_SIZE = (48, 32), 32
X_PIECE, PIECE = 80, 144
BASES = (0, 192, 320, 448, 576)
INVERSE, STARTS = N_CTX, N_CTX + 1


def dot(left, right):
    return jnp.dot(left, right, preferred_element_type=F32)


def dot_nt(left, right):
    return lax.dot_general(left, right, (((1,), (1,)), ((), ())), preferred_element_type=F32)


def remote(src, dst, send, recv, device):
    return pltpu.make_async_remote_copy(
        src_ref=src, dst_ref=dst, send_sem=send, recv_sem=recv, device_id=device, device_id_type=MESH
    )


def kernel(
    latent, positions, docs, query, d_out, d_query, d_latent,
    q_in, g_in, g_wide, q_rows, q_cols, g_rows, g_cols, blocks, places, info, table,
    keys, score, grad_p, prob, grad_s, dkv, dq,
    x_part0, y_part0, x_part1, y_part1, x_twin0, y_twin0, x_twin1, y_twin1,
    x_recv0, y_recv0, x_recv1, y_recv1, x_sum, y_sum,
    x_last, y_last, piece, pieces, raw, total_rows, docs_in,
    in_sem, info_sem, a_send, a_recv, b_send, b_recv, c_send, c_recv, pos_send, pos_recv,
    t_send, t_recv, x_send, x_got, y_send, y_got, xl_send, xl_got, yl_send, yl_got, o_send, o_recv,
):
    ctx, tp = lax.axis_index("ctx"), lax.axis_index("tp")
    core, group = lax.rem(ctx, 2), ctx // 2
    x, low_z = tp // 2, lax.rem(tp, 2)

    def turn(index, step, size):
        return lax.rem(index + step + size, size)

    def along_x(step):
        return (ctx, 2 * turn(x, step, 4) + low_z)

    y, high_z = group // 2, lax.rem(group, 2)
    me = 8 * core + group
    twin = (2 * group + 1 - core, tp)
    mates, targets, sources = [], [], []
    for k in range(1, 8):
        flip, step = k // 4, k % 4
        over = 1 - high_z if flip else high_z
        targets.append(2 * turn(y, step, 4) + over)
        sources.append(2 * turn(y, -step, 4) + over)
        mates.append((2 * targets[-1] + core, 2 * x + (1 - low_z if flip else low_z)))
    over_tp = [(ctx, turn(tp, k, N_TP)) for k in range(1, N_TP)]
    plane = [
        (2 * turn(group, k, 8) + core, 2 * x + turn(low_z, j, 2))
        for j in range(2) for k in range(8) if j or k
    ]

    friends = mates + [twin, along_x(1), along_x(-1), plane[7]]
    barrier = pltpu.get_barrier_semaphore()
    for device in friends:
        pl.semaphore_signal(barrier, inc=1, device_id=device, device_id_type=MESH)
    loads = [
        pltpu.make_async_copy(positions, places.at[core, group], in_sem.at[3]),
        pltpu.make_async_copy(latent, raw, in_sem.at[0]),
        pltpu.make_async_copy(query, q_in, in_sem.at[1]),
        pltpu.make_async_copy(d_out, g_in, in_sem.at[2]),
        pltpu.make_async_copy(docs, docs_in, in_sem.at[4]),
    ]
    for copy in loads:
        copy.start()
    loads[0].wait()
    swapped = jnp.broadcast_to(places[core, group][:, :1] // RUN % 2 == 1, (WIDTH, TOK))

    def even_first(value):
        value = value.astype(F32)
        return jnp.where(swapped, pltpu.roll(value, RUN, 1), value).astype(BF16)

    loads[1].wait()
    blocks[me] = even_first(raw[...])
    pl.semaphore_wait(barrier, len(friends))

    def quarter(index):
        return pl.ds(pl.multiple_of(QUARTER * index, 16), QUARTER)

    first, small = [], []
    for j in range(2):
        for k, device in enumerate(mates):
            part = blocks.at[me, quarter(turn(x, j, 4))]
            copy = remote(part, part, a_send.at[2 * k + j], a_recv.at[2 * k + j], device)
            copy.start()
            first.append(copy)
    for k, device in enumerate(mates):
        here = places.at[core, group]
        copy = remote(here, here, pos_send.at[k], pos_recv.at[k], device)
        copy.start()
        small.append(copy)
    to_twin = [remote(blocks.at[me], blocks.at[me], c_send.at[7], c_recv.at[7], twin)]
    to_twin[0].start()

    loads[2].wait()
    for h in range(HEADS):
        rows = q_in[h].T
        for run in range(2):
            q_rows[run, RUN * h : RUN * (h + 1), :] = rows[RUN * run : RUN * (run + 1)]

    second = []
    for j in range(2):
        for k in range(7):
            part = blocks.at[8 * core + sources[k], quarter(turn(x, j, 4))]
            at = 2 * k + j
            remote(part, part, a_send.at[at], a_recv.at[at], mates[k]).wait_recv()
            copy = remote(part, part, b_send.at[at], b_recv.at[at], along_x(1 - 2 * j))
            copy.start()
            second.append(copy)
    for k in range(7):
        here = places.at[core, sources[k]]
        remote(here, here, pos_send.at[k], pos_recv.at[k], mates[k]).wait_recv()
    here = places.at[core]
    copy = remote(here, here, pos_send.at[7], pos_recv.at[7], twin)
    copy.start()
    small.append(copy)

    for run in range(2):
        for part in range(ROWS // 128):
            pair = slice(128 * part, 128 * (part + 1))
            q_cols[run, :, pair] = q_rows[run, pair, :].T
    loads[3].wait()
    for part in range(LAT // 128):
        lanes = slice(128 * part, 128 * (part + 1))
        g_wide[part] = g_in[:, lanes].astype(F32)
        for h in range(HEADS):
            rows = g_wide[part, pl.ds(h, TOK, HEADS), :].astype(BF16)
            for run in range(2):
                g_rows[run, RUN * h : RUN * (h + 1), lanes] = rows[RUN * run : RUN * (run + 1)]
    for run in range(2):
        for part in range(ROWS // 128):
            pair = slice(128 * part, 128 * (part + 1))
            g_cols[run, :, pair] = g_rows[run, pair, :].T

    here = places.at[1 - core]
    remote(here, here, pos_send.at[7], pos_recv.at[7], twin).wait_recv()
    lane = lax.broadcasted_iota(I32, (N_CTX, TOK), 1)
    row = lax.broadcasted_iota(I32, (N_CTX, TOK), 0)
    at = jnp.concatenate([places[d // 8, d % 8] for d in range(N_CTX)], axis=0)
    one, two = at[:, :1] // RUN, at[:, RUN : RUN + 1] // RUN
    holder = jnp.where((one == lane) | (two == lane), row, 0)
    info[:N_CTX] = at
    info[INVERSE : INVERSE + 1] = jnp.sum(holder, axis=0, keepdims=True)
    loads[4].wait()
    for value in range(1, N_DOCS):
        count = jnp.sum((docs_in[...] < value).astype(I32), keepdims=True)
        info[STARTS + value - 1 : STARTS + value] = jnp.broadcast_to(count, (1, TOK))
    copy = pltpu.make_async_copy(info, table, info_sem)
    copy.start()
    copy.wait()

    for k in range(7):
        block = blocks.at[8 * core + sources[k]]
        for j in range(2):
            part = blocks.at[8 * core + sources[k], quarter(turn(x, 3 - j, 4))]
            at = 2 * k + j
            remote(part, part, b_send.at[at], b_recv.at[at], along_x(1 - 2 * j)).wait_recv()
        copy = remote(block, block, c_send.at[k], c_recv.at[k], twin)
        copy.start()
        to_twin.append(copy)
    for copy in first + second + to_twin + small:
        copy.wait_send()
    for k in range(8):
        block = blocks.at[8 * (1 - core) + (sources + [group])[k]]
        remote(block, block, c_send.at[k], c_recv.at[k], twin).wait_recv()

    bounds = [table[STARTS + index, 0] for index in range(N_DOCS - 1)]
    low = lax.broadcasted_iota(I32, (WIDTH, TOK), 1) < RUN
    bases = [table[me, RUN * run] for run in range(2)]
    tops = [base // TOK - (SLOTS - 1) for base in bases]

    for run in range(2):
        for slot in range(SLOTS):
            tile = jnp.clip(tops[run] + slot, 0, N_CTX - 1)
            one, two = (jnp.clip(table[INVERSE, 2 * tile + i], 0, N_CTX - 1) for i in range(2))
            keys[run, :, TOK * slot : TOK * (slot + 1)] = jnp.where(low, blocks[one], blocks[two])

        position = bases[run] + lax.broadcasted_iota(I32, (ROWS, 1), 0) % RUN
        begin = jnp.zeros((ROWS, 1), I32)
        for bound in bounds:
            begin = jnp.where(position >= bound, bound, begin)
        begin = begin - tops[run] * TOK
        position = position - tops[run] * TOK

        peak = jnp.full((ROWS, TOK), -1e30, F32)
        for start in range(0, SPAN, 2 * TOK):
            size = min(2 * TOK, SPAN - start)
            columns = slice(start, start + size)
            key = start + lax.broadcasted_iota(I32, (ROWS, size), 1)
            allowed = key >= begin
            if start + size == SPAN:
                allowed = allowed & (key <= position)
            value = jnp.where(allowed, dot(q_rows[run], keys[run, :, columns]), -1e30)
            score[:, columns] = value
            grad_p[:, columns] = dot(g_rows[run], keys[run, :LAT, columns])
            for part in range(size // TOK):
                peak = jnp.maximum(peak, value[:, TOK * part : TOK * (part + 1)])
        peak = jnp.max(peak, axis=1, keepdims=True) * (SCALE * LOG2E)

        sums = jnp.zeros((ROWS, TOK), F32)
        mixed = jnp.zeros((ROWS, TOK), F32)
        for slot in range(SLOTS):
            columns = slice(TOK * slot, TOK * (slot + 1))
            weight = jnp.exp2(score[:, columns] * (SCALE * LOG2E) - peak)
            score[:, columns] = weight
            sums = sums + weight
            mixed = mixed + weight * grad_p[:, columns]
        inverse = 1.0 / jnp.sum(sums, axis=1, keepdims=True)
        delta = jnp.sum(mixed, axis=1, keepdims=True) * inverse
        scaled = inverse * SCALE
        for slot in range(SLOTS):
            columns = slice(TOK * slot, TOK * (slot + 1))
            weight = score[:, columns]
            prob[run, :, columns] = (weight * inverse).astype(BF16)
            grad_s[run, :, columns] = (weight * scaled * (grad_p[:, columns] - delta)).astype(BF16)

    def gradient(rows, target):
        size = rows.stop - rows.start
        values = slice(rows.start, min(rows.stop, LAT))
        for run in range(2):
            for start in range(0, SPAN, 2 * TOK):
                width = min(2 * TOK, SPAN - start)
                columns = slice(start, start + width)
                both = dot(q_cols[run, rows, :], grad_s[run, :, columns])
                value = dot(g_cols[run, values, :], prob[run, :, columns])
                if values.stop < rows.stop:
                    value = jnp.concatenate(
                        [value, jnp.zeros((rows.stop - values.stop, width), F32)], axis=0
                    )
                both = both + value
                for part in range(width // TOK):
                    dkv[run, start // TOK + part, :size] = both[:, TOK * part : TOK * (part + 1)]
        first_lanes = lax.broadcasted_iota(I32, (size, TOK), 1) < RUN
        for device in range(N_CTX):
            out = []
            runs = [table[device, RUN * half] // RUN for half in range(2)]
            for parity in range(2):
                tile = jnp.where(runs[0] % 2 == parity, runs[0], runs[1]) // 2
                found = jnp.zeros((size, TOK), F32)
                for run in range(2):
                    slot = tile - tops[run]
                    inside = (slot >= 0) & (slot < SLOTS)
                    term = dkv[run, jnp.clip(slot, 0, SLOTS - 1), :size]
                    found = found + jnp.where(inside, term, 0.0)
                out.append(found)
            target[device // 8, device % 8] = jnp.where(first_lanes, out[0], out[1]).astype(BF16)

    def query_gradient(run):
        dq[run] = dot_nt(grad_s[run], keys[run])

    def rows_of(index, size):
        return pl.ds(pl.multiple_of(size * index, 16), size)

    swaps, x_step, y_step = [], [], []
    chip = [x_part0, y_part0, x_part1, y_part1]
    twin_part = [x_twin0, y_twin0, x_twin1, y_twin1]
    x_recv = [x_recv0, x_recv1]
    y_recv = [y_recv0, y_recv1]

    def to_twin_core(c):
        copy = remote(chip[c].at[1 - core], twin_part[c], t_send.at[c], t_recv.at[c], twin)
        copy.start()
        swaps.append(copy)

    def over_links(c):
        swaps[c].wait_recv()
        ours = chip[c]
        for g in range(8):
            ours[core, g] = (ours[core, g].astype(F32) + twin_part[c][g].astype(F32)).astype(BF16)
        half = c // 2
        if c % 2 == 0:
            size = X_SIZES[half]
            for k in range(3):
                source = ours.at[core, :, rows_of(turn(x, k + 1, 4), size)]
                at = 3 * half + k
                copy = remote(source, x_recv[half].at[k], x_send.at[at], x_got.at[at], along_x(k + 1))
                copy.start()
                x_step.append(copy)
        else:
            for k in range(7):
                source = ours.at[core, targets[k]]
                at = 7 * half + k
                copy = remote(source, y_recv[half].at[k], y_send.at[at], y_got.at[at], mates[k])
                copy.start()
                y_step.append(copy)

    for c in range(4):
        gradient(slice(BASES[c], BASES[c + 1]), chip[c])
        to_twin_core(c)
        if c:
            over_links(c - 1)
    over_links(3)

    for run in range(2):
        query_gradient(run)
    for h in range(HEADS):
        rows = slice(RUN * h, RUN * (h + 1))
        both = jnp.concatenate([dq[0, rows, :], dq[1, rows, :]], axis=0)
        q_in[h] = both.T.astype(BF16)
    store = pltpu.make_async_copy(q_in, d_query, in_sem.at[2])
    store.start()

    for copy in x_step:
        copy.wait_recv()
    for half in range(2):
        size, first_row = X_SIZES[half], half * X_SIZES[0]
        for g in range(8):
            total = chip[2 * half][core, g, rows_of(x, size), :].astype(F32)
            for k in range(3):
                total = total + x_recv[half][k, g].astype(F32)
            x_sum[g, first_row : first_row + size] = total.astype(BF16)
    x_end = []
    for k, device in enumerate(plane):
        copy = remote(
            x_sum.at[turn(group, (k + 1) % 8, 8)], x_last.at[k], xl_send.at[k], xl_got.at[k], device
        )
        copy.start()
        x_end.append(copy)
    for copy in y_step:
        copy.wait_recv()
    for half in range(2):
        total = chip[2 * half + 1][core, group].astype(F32)
        for k in range(7):
            total = total + y_recv[half][k].astype(F32)
        y_sum[half] = total.astype(BF16)
    y_end = []
    for k, device in enumerate(over_tp):
        source = y_sum.at[:, rows_of(turn(tp, k + 1, N_TP) // 2, Y_SIZE)]
        copy = remote(source, y_last.at[k], yl_send.at[k], yl_got.at[k], device)
        copy.start()
        y_end.append(copy)

    for copy in x_end:
        copy.wait_recv()
    total = x_sum[group].astype(F32)
    for k in range(15):
        total = total + x_last[k].astype(F32)
    piece[:X_PIECE] = total.astype(BF16)
    for copy in y_end:
        copy.wait_recv()
    for half in range(2):
        total = y_sum[half, rows_of(x, Y_SIZE), :].astype(F32)
        for k in range(7):
            total = total + y_last[k, half].astype(F32)
        piece[X_PIECE + half * Y_SIZE : X_PIECE + (half + 1) * Y_SIZE] = total.astype(BF16)
    out_step = []
    for k in range(3):
        copy = remote(piece, pieces.at[k], o_send.at[k], o_recv.at[k], along_x(k + 1))
        copy.start()
        out_step.append(copy)

    def place(index, value):
        first_row = 0
        for c in (0, 2, 1, 3):
            size = X_SIZES[c // 2] if c % 2 == 0 else Y_SIZE
            at = pl.ds(pl.multiple_of(BASES[c] + size * index, 16), size)
            total_rows[at, :] = value[first_row : first_row + size]
            first_row += size

    place(x, piece[...])
    for k in range(3):
        out_step[k].wait_recv()
        place(turn(x, -(k + 1), 4), pieces[k])
    d_latent[...] = even_first(total_rows[...])
    store.wait()
    for copy in swaps + x_step + y_step + x_end + y_end + out_step:
        copy.wait_send()


def local(query, latent, d_out, positions, doc_ids):
    whole, fast = pl.BlockSpec(memory_space=pl.ANY), pl.BlockSpec(memory_space=pltpu.VMEM)
    vmem, dma = pltpu.VMEM, pltpu.SemaphoreType.DMA
    d_query, d_latent = pl.pallas_call(
        kernel,
        out_shape=[
            jax.ShapeDtypeStruct((HEADS, WIDTH, TOK), BF16),
            jax.ShapeDtypeStruct((WIDTH, TOK), BF16),
        ],
        in_specs=[whole] * 5,
        out_specs=[whole, fast],
        scratch_shapes=[
            vmem((HEADS, WIDTH, TOK), BF16),
            vmem((TOK * HEADS, LAT), BF16),
            vmem((LAT // 128, TOK * HEADS, 128), F32),
            vmem((2, ROWS, WIDTH), BF16),
            vmem((2, WIDTH, ROWS), BF16),
            vmem((2, ROWS, LAT), BF16),
            vmem((2, LAT, ROWS), BF16),
            vmem((N_CTX, WIDTH, TOK), BF16),
            vmem((2, 8, 1, TOK), I32),
            vmem((24, TOK), I32),
            pltpu.SMEM((24, TOK), I32),
            vmem((2, WIDTH, SPAN), BF16),
            vmem((ROWS, SPAN), F32),
            vmem((ROWS, SPAN), F32),
            vmem((2, ROWS, SPAN), BF16),
            vmem((2, ROWS, SPAN), BF16),
            vmem((2, SLOTS, BASES[1], TOK), F32),
            vmem((2, ROWS, WIDTH), F32),
        ]
        + [vmem((2, 8, BASES[c + 1] - BASES[c], TOK), BF16) for c in range(4)]
        + [vmem((8, BASES[c + 1] - BASES[c], TOK), BF16) for c in range(4)]
        + [
            vmem((3, 8, X_SIZES[0], TOK), BF16),
            vmem((7, 4 * Y_SIZE, TOK), BF16),
            vmem((3, 8, X_SIZES[1], TOK), BF16),
            vmem((7, 4 * Y_SIZE, TOK), BF16),
            vmem((8, X_PIECE, TOK), BF16),
            vmem((2, 4 * Y_SIZE, TOK), BF16),
            vmem((15, X_PIECE, TOK), BF16),
            vmem((7, 2, Y_SIZE, TOK), BF16),
            vmem((PIECE, TOK), BF16),
            vmem((3, PIECE, TOK), BF16),
            vmem((WIDTH, TOK), BF16),
            vmem((WIDTH, TOK), BF16),
            vmem((N_CTX, TOK), I32),
            dma((5,)),
            dma,
        ]
        + [dma((size,)) for size in (14, 14, 8, 8, 4, 6, 14, 15, 7, 3) for _ in range(2)],
        compiler_params=pltpu.CompilerParams(
            collective_id=0, has_side_effects=True, vmem_limit_bytes=63 << 20
        ),
        name="latent_attention_backward",
    )(
        latent.T,
        positions.reshape(1, TOK),
        doc_ids.reshape(-1, TOK),
        query.transpose(1, 2, 0),
        d_out.reshape(TOK * HEADS, LAT),
    )
    return (d_query.transpose(2, 0, 1), d_latent.T)


def solution(mesh):
    return jax.shard_map(
        local,
        mesh=mesh,
        in_specs=(P("ctx", "tp", None), P("ctx", None), P("ctx", "tp", None), P("ctx"), P()),
        out_specs=(P("ctx", "tp", None), P("ctx", None)),
        check_vma=False,
    )
```

time: 64.2 us -> 58.7 us (0.914)
  Pallas kernels: 60.3 us -> 54.8 us
    pallas_call x1, Pallas kernels: 60.3 us -> 54.8 us  [local(): pl.pallas_call(kernel, out_shape=[jax.ShapeDtypeStruct((HEADS, WIDTH, TOK...]
where the time goes in v3:
time: 58.7 us; the launch traced here: 58.5 us
  Pallas kernels  54.8 us (93%)
  local copies, waits for them, and re-layouts  3.07 us (5%)
  between operations  0.65 us (1%)
    pallas_call x1, Pallas kernels, local(): pl.pallas_call(kernel, out_shape=[jax.ShapeDtypeStruct((HEADS, WIDTH, TOK...  54.8 us
    unnamed x4, local copies, waits for them, and re-layouts  3.07 us

profile of v3, /device:TPU:0, one launch (start us, length us, event | category | flops | bytes accessed | tf_op | source)
XLA Modules:
  0.0 58.5 jit_solution(15455303197479027004)
XLA Ops:
  0.6 54.8 %latent_attention_backward.1 = (bf16[8,576,128]{2,1,0:T(8,128)(2,1)}, bf16[576,128]{1,0:T(8,128)(2,1)}) custom-call(bf16[576,128]{1,0:T(8,128)(2,1)} %bitcast.11, s32[1,128]{1,0:T(1,128)} %bitcast.13, s32[16,128]{1,0:T(8,128)} %bitcast.12, bf16[8,576,128]{2,1,0:T(8,128)(2,1)} %bitcast.8, bf16[1024,512]{1,0:T(8,128)(2,1)} %bitcast.9), custom_call_target="tpu_custom_call" | custom-call | tf_op jit(solution)/shard_map/latent_attention_backward/pallas_call | solution.py:394
  55.4 0.0 copy-start
  55.4 2.4 %copy.9 = bf16[128,8,576]{0,2,1:T(8,128)(2,1)} copy(bf16[128,8,576]{0,2,1:T(8,128)(2,1)} %bitcast.7) | data formatting | bytes 2359296
  57.8 0.0 copy-done
  57.8 0.7 %copy.10 = bf16[128,576]{0,1:T(8,128)(2,1)} copy(bf16[128,576]{0,1:T(8,128)(2,1)S(1)} %bitcast.10) | data formatting | bytes 294912
Async XLA Ops:
  55.4 2.4 %copy-start = (bf16[576,128]{1,0:T(8,128)(2,1)S(1)}, bf16[576,128]{1,0:T(8,128)(2,1)}, u32[]{:S(2)}) copy-start(bf16[576,128]{1,0:T(8,128)(2,1)} %get-tuple-element.5) | copy-start | bytes 442372

commit v4 on v3

--- a/solution.py
+++ b/solution.py
@@ -15,9 +15,10 @@
 SLOTS = 9
 SPAN = SLOTS * TOK
 QUARTER = WIDTH // 4
-X_SIZES, Y_SIZE = (48, 32), 32
-X_PIECE, PIECE = 80, 144
-BASES = (0, 192, 320, 448, 576)
+X_SIZES, Y_SIZE = (32, 48), 32
+X_BOTH, X_PIECE, PIECE = 80, 48, 80
+BASES = (0, 128, 256, 448, 576)
+CHUNK = 192
 INVERSE, STARTS = N_CTX, N_CTX + 1
 
 
@@ -36,12 +37,12 @@
 
 
 def kernel(
-    latent, positions, docs, query, d_out, d_query, d_latent,
+    latent, positions, docs, query, d_out, d_query, pieces,
     q_in, g_in, g_wide, q_rows, q_cols, g_rows, g_cols, blocks, places, info, table,
     keys, score, grad_p, prob, grad_s, dkv, dq,
     x_part0, y_part0, x_part1, y_part1, x_twin0, y_twin0, x_twin1, y_twin1,
     x_recv0, y_recv0, x_recv1, y_recv1, x_sum, y_sum,
-    x_last, y_last, piece, pieces, raw, total_rows, docs_in,
+    x_last, y_last, piece, raw, docs_in,
     in_sem, info_sem, a_send, a_recv, b_send, b_recv, c_send, c_recv, pos_send, pos_recv,
     t_send, t_recv, x_send, x_got, y_send, y_got, xl_send, xl_got, yl_send, yl_got, o_send, o_recv,
 ):
@@ -85,22 +86,17 @@
     for copy in loads:
         copy.start()
     loads[0].wait()
-    swapped = jnp.broadcast_to(places[core, group][:, :1] // RUN % 2 == 1, (WIDTH, TOK))
-
-    def even_first(value):
-        value = value.astype(F32)
-        return jnp.where(swapped, pltpu.roll(value, RUN, 1), value).astype(BF16)
-
     loads[1].wait()
-    blocks[me] = even_first(raw[...])
+    blocks[me] = even_first(raw[...], places[core, group])
     pl.semaphore_wait(barrier, len(friends))
 
     def quarter(index):
         return pl.ds(pl.multiple_of(QUARTER * index, 16), QUARTER)
 
     first, small = [], []
-    for j in range(2):
+    for turn_of in range(2):
         for k, device in enumerate(mates):
+            j = (turn_of + k) % 2
             part = blocks.at[me, quarter(turn(x, j, 4))]
             copy = remote(part, part, a_send.at[2 * k + j], a_recv.at[2 * k + j], device)
             copy.start()
@@ -110,7 +106,7 @@
         copy = remote(here, here, pos_send.at[k], pos_recv.at[k], device)
         copy.start()
         small.append(copy)
-    to_twin = [remote(blocks.at[me], blocks.at[me], c_send.at[7], c_recv.at[7], twin)]
+    to_twin = [remote(blocks.at[me], blocks.at[me], c_send.at[28], c_recv.at[28], twin)]
     to_twin[0].start()
 
     loads[2].wait()
@@ -119,15 +115,24 @@
         for run in range(2):
             q_rows[run, RUN * h : RUN * (h + 1), :] = rows[RUN * run : RUN * (run + 1)]
 
+    def share(k, i, block, index):
+        part = block.at[quarter(index)]
+        copy = remote(part, part, c_send.at[4 * k + i], c_recv.at[4 * k + i], twin)
+        copy.start()
+        to_twin.append(copy)
+
     second = []
-    for j in range(2):
+    for turn_of in range(2):
         for k in range(7):
-            part = blocks.at[8 * core + sources[k], quarter(turn(x, j, 4))]
+            j = (turn_of + k) % 2
+            block = blocks.at[8 * core + sources[k]]
+            part = block.at[quarter(turn(x, j, 4))]
             at = 2 * k + j
             remote(part, part, a_send.at[at], a_recv.at[at], mates[k]).wait_recv()
             copy = remote(part, part, b_send.at[at], b_recv.at[at], along_x(1 - 2 * j))
             copy.start()
             second.append(copy)
+            share(k, j, block, turn(x, j, 4))
     for k in range(7):
         here = places.at[core, sources[k]]
         remote(here, here, pos_send.at[k], pos_recv.at[k], mates[k]).wait_recv()
@@ -170,20 +175,23 @@
     copy.start()
     copy.wait()
 
-    for k in range(7):
-        block = blocks.at[8 * core + sources[k]]
-        for j in range(2):
-            part = blocks.at[8 * core + sources[k], quarter(turn(x, 3 - j, 4))]
+    for turn_of in range(2):
+        for k in range(7):
+            j = (turn_of + k) % 2
+            block = blocks.at[8 * core + sources[k]]
+            part = block.at[quarter(turn(x, 3 - j, 4))]
             at = 2 * k + j
             remote(part, part, b_send.at[at], b_recv.at[at], along_x(1 - 2 * j)).wait_recv()
-        copy = remote(block, block, c_send.at[k], c_recv.at[k], twin)
-        copy.start()
-        to_twin.append(copy)
+            share(k, 3 - j, block, turn(x, 3 - j, 4))
     for copy in first + second + to_twin + small:
         copy.wait_send()
-    for k in range(8):
-        block = blocks.at[8 * (1 - core) + (sources + [group])[k]]
-        remote(block, block, c_send.at[k], c_recv.at[k], twin).wait_recv()
+    for k in range(7):
+        block = blocks.at[8 * (1 - core) + sources[k]]
+        for i in range(4):
+            part = block.at[quarter(turn(x, i, 4))]
+            remote(part, part, c_send.at[4 * k + i], c_recv.at[4 * k + i], twin).wait_recv()
+    block = blocks.at[8 * (1 - core) + group]
+    remote(block, block, c_send.at[28], c_recv.at[28], twin).wait_recv()
 
     bounds = [table[STARTS + index, 0] for index in range(N_DOCS - 1)]
     low = lax.broadcasted_iota(I32, (WIDTH, TOK), 1) < RUN
@@ -257,13 +265,12 @@
             runs = [table[device, RUN * half] // RUN for half in range(2)]
             for parity in range(2):
                 tile = jnp.where(runs[0] % 2 == parity, runs[0], runs[1]) // 2
-                found = jnp.zeros((size, TOK), F32)
+                found = []
                 for run in range(2):
                     slot = tile - tops[run]
                     inside = (slot >= 0) & (slot < SLOTS)
-                    term = dkv[run, jnp.clip(slot, 0, SLOTS - 1), :size]
-                    found = found + jnp.where(inside, term, 0.0)
-                out.append(found)
+                    found.append(dkv[run, jnp.where(inside, slot, SLOTS), :size])
+                out.append(found[0] + found[1])
             target[device // 8, device % 8] = jnp.where(first_lanes, out[0], out[1]).astype(BF16)
 
     def query_gradient(run):
@@ -305,6 +312,7 @@
                 copy.start()
                 y_step.append(copy)
 
+    dkv[:, SLOTS] = jnp.zeros((2, CHUNK, TOK), F32)
     for c in range(4):
         gradient(slice(BASES[c], BASES[c + 1]), chip[c])
         to_twin_core(c)
@@ -330,11 +338,13 @@
             for k in range(3):
                 total = total + x_recv[half][k, g].astype(F32)
             x_sum[g, first_row : first_row + size] = total.astype(BF16)
+    def window(index):
+        return pl.ds(pl.multiple_of(X_SIZES[0] * index, 16), X_PIECE)
+
     x_end = []
     for k, device in enumerate(plane):
-        copy = remote(
-            x_sum.at[turn(group, (k + 1) % 8, 8)], x_last.at[k], xl_send.at[k], xl_got.at[k], device
-        )
+        source = x_sum.at[turn(group, (k + 1) % 8, 8), window(turn(low_z, (k + 1) // 8, 2))]
+        copy = remote(source, x_last.at[k], xl_send.at[k], xl_got.at[k], device)
         copy.start()
         x_end.append(copy)
     for copy in y_step:
@@ -346,59 +356,88 @@
         y_sum[half] = total.astype(BF16)
     y_end = []
     for k, device in enumerate(over_tp):
-        source = y_sum.at[:, rows_of(turn(tp, k + 1, N_TP) // 2, Y_SIZE)]
+        other = turn(tp, k + 1, N_TP)
+        source = y_sum.at[lax.rem(other, 2), rows_of(other // 2, Y_SIZE)]
         copy = remote(source, y_last.at[k], yl_send.at[k], yl_got.at[k], device)
         copy.start()
         y_end.append(copy)
 
     for copy in x_end:
         copy.wait_recv()
-    total = x_sum[group].astype(F32)
+    total = x_sum[group, window(low_z), :].astype(F32)
     for k in range(15):
         total = total + x_last[k].astype(F32)
     piece[:X_PIECE] = total.astype(BF16)
     for copy in y_end:
         copy.wait_recv()
-    for half in range(2):
-        total = y_sum[half, rows_of(x, Y_SIZE), :].astype(F32)
-        for k in range(7):
-            total = total + y_last[k, half].astype(F32)
-        piece[X_PIECE + half * Y_SIZE : X_PIECE + (half + 1) * Y_SIZE] = total.astype(BF16)
+    total = y_sum[low_z, rows_of(x, Y_SIZE), :].astype(F32)
+    for k in range(7):
+        total = total + y_last[k].astype(F32)
+    piece[X_PIECE:] = total.astype(BF16)
+    keep = pltpu.make_async_copy(piece, pieces.at[tp], in_sem.at[0])
+    keep.start()
     out_step = []
-    for k in range(3):
-        copy = remote(piece, pieces.at[k], o_send.at[k], o_recv.at[k], along_x(k + 1))
+    for k, device in enumerate(over_tp):
+        copy = remote(piece, pieces.at[tp], o_send.at[k], o_recv.at[k], device)
         copy.start()
         out_step.append(copy)
-
-    def place(index, value):
-        first_row = 0
-        for c in (0, 2, 1, 3):
-            size = X_SIZES[c // 2] if c % 2 == 0 else Y_SIZE
-            at = pl.ds(pl.multiple_of(BASES[c] + size * index, 16), size)
-            total_rows[at, :] = value[first_row : first_row + size]
-            first_row += size
-
-    place(x, piece[...])
-    for k in range(3):
-        out_step[k].wait_recv()
-        place(turn(x, -(k + 1), 4), pieces[k])
-    d_latent[...] = even_first(total_rows[...])
+    for k, device in enumerate(over_tp):
+        other = pieces.at[turn(tp, -(k + 1), N_TP)]
+        remote(other, other, o_send.at[k], o_recv.at[k], device).wait_recv()
+    keep.wait()
     store.wait()
     for copy in swaps + x_step + y_step + x_end + y_end + out_step:
         copy.wait_send()
 
 
+def even_first(value, here):
+    swapped = jnp.broadcast_to(here[:, :1] // RUN % 2 == 1, value.shape)
+    value = value.astype(F32)
+    return jnp.where(swapped, pltpu.roll(value, RUN, 1), value).astype(BF16)
+
+
+def finish(d_query, pieces, positions, query_out, latent_out, held, parts, place, whole, in_sem, out_sem):
+    loads = [
+        pltpu.make_async_copy(pieces, parts, in_sem.at[HEADS]),
+        pltpu.make_async_copy(positions, place, in_sem.at[HEADS + 1]),
+    ]
+    for h in range(HEADS):
+        loads.append(pltpu.make_async_copy(d_query.at[h], held.at[h], in_sem.at[h]))
+    for copy in loads:
+        copy.start()
+    stores = []
+    for h in range(HEADS):
+        loads[2 + h].wait()
+        stores.append(pltpu.make_async_copy(held.at[h], query_out.at[h], out_sem.at[h]))
+        stores[-1].start()
+    loads[0].wait()
+    loads[1].wait()
+    for x in range(N_TP // 2):
+        for low_z in range(2):
+            size = X_SIZES[low_z]
+            at = BASES[2 * low_z] + size * x
+            whole[at : at + size, :] = parts[2 * x + low_z, :size]
+            at = BASES[2 * low_z + 1] + Y_SIZE * x
+            whole[at : at + Y_SIZE, :] = parts[2 * x + low_z, X_PIECE:]
+    whole[...] = even_first(whole[...], place[...])
+    stores.append(pltpu.make_async_copy(whole, latent_out, out_sem.at[HEADS]))
+    stores[-1].start()
+    for copy in stores:
+        copy.wait()
+
+
 def local(query, latent, d_out, positions, doc_ids):
-    whole, fast = pl.BlockSpec(memory_space=pl.ANY), pl.BlockSpec(memory_space=pltpu.VMEM)
+    whole = pl.BlockSpec(memory_space=pl.ANY)
     vmem, dma = pltpu.VMEM, pltpu.SemaphoreType.DMA
-    d_query, d_latent = pl.pallas_call(
+    here = positions.reshape(1, TOK)
+    d_query, pieces = pl.pallas_call(
         kernel,
         out_shape=[
             jax.ShapeDtypeStruct((HEADS, WIDTH, TOK), BF16),
-            jax.ShapeDtypeStruct((WIDTH, TOK), BF16),
+            jax.ShapeDtypeStruct((N_TP, PIECE, TOK), BF16),
         ],
         in_specs=[whole] * 5,
-        out_specs=[whole, fast],
+        out_specs=[whole, whole],
         scratch_shapes=[
             vmem((HEADS, WIDTH, TOK), BF16),
             vmem((TOK * HEADS, LAT), BF16),
@@ -416,7 +455,7 @@
             vmem((ROWS, SPAN), F32),
             vmem((2, ROWS, SPAN), BF16),
             vmem((2, ROWS, SPAN), BF16),
-            vmem((2, SLOTS, BASES[1], TOK), F32),
+            vmem((2, SLOTS + 1, CHUNK, TOK), F32),
             vmem((2, ROWS, WIDTH), F32),
         ]
         + [vmem((2, 8, BASES[c + 1] - BASES[c], TOK), BF16) for c in range(4)]
@@ -426,30 +465,47 @@
             vmem((7, 4 * Y_SIZE, TOK), BF16),
             vmem((3, 8, X_SIZES[1], TOK), BF16),
             vmem((7, 4 * Y_SIZE, TOK), BF16),
-            vmem((8, X_PIECE, TOK), BF16),
+            vmem((8, X_BOTH, TOK), BF16),
             vmem((2, 4 * Y_SIZE, TOK), BF16),
             vmem((15, X_PIECE, TOK), BF16),
-            vmem((7, 2, Y_SIZE, TOK), BF16),
+            vmem((7, Y_SIZE, TOK), BF16),
             vmem((PIECE, TOK), BF16),
-            vmem((3, PIECE, TOK), BF16),
-            vmem((WIDTH, TOK), BF16),
             vmem((WIDTH, TOK), BF16),
             vmem((N_CTX, TOK), I32),
             dma((5,)),
             dma,
         ]
-        + [dma((size,)) for size in (14, 14, 8, 8, 4, 6, 14, 15, 7, 3) for _ in range(2)],
+        + [dma((size,)) for size in (14, 14, 29, 8, 4, 6, 14, 15, 7, 7) for _ in range(2)],
         compiler_params=pltpu.CompilerParams(
             collective_id=0, has_side_effects=True, vmem_limit_bytes=63 << 20
         ),
         name="latent_attention_backward",
     )(
         latent.T,
-        positions.reshape(1, TOK),
+        here,
         doc_ids.reshape(-1, TOK),
         query.transpose(1, 2, 0),
         d_out.reshape(TOK * HEADS, LAT),
     )
+    d_query, d_latent = pl.pallas_call(
+        finish,
+        out_shape=[
+            jax.ShapeDtypeStruct((HEADS, WIDTH, TOK), BF16),
+            jax.ShapeDtypeStruct((WIDTH, TOK), BF16),
+        ],
+        in_specs=[whole] * 3,
+        out_specs=[whole] * 2,
+        scratch_shapes=[
+            vmem((HEADS, WIDTH, TOK), BF16),
+            vmem((N_TP, PIECE, TOK), BF16),
+            vmem((1, TOK), I32),
+            vmem((WIDTH, TOK), BF16),
+            dma((HEADS + 2,)),
+            dma((HEADS + 1,)),
+        ],
+        compiler_params=pltpu.CompilerParams(vmem_limit_bytes=63 << 20),
+        name="finish",
+    )(d_query, pieces, here)
     return (d_query.transpose(2, 0, 1), d_latent.T)
 
 

time: 58.7 us -> 55.6 us (0.947)
  local copies, waits for them, and re-layouts: 3.07 us -> 0 us
    unnamed x4 -> x0, local copies, waits for them, and re-layouts: 3.07 us -> none
    pallas_call x1, Pallas kernels: 54.8 us -> 52.3 us  [local(): pl.pallas_call(kernel, out_shape=[jax.ShapeDtypeStruct((HEADS, WIDTH, TOK...]
    pallas_call x0 -> x1, Pallas kernels: none -> 2.36 us  [local(): pl.pallas_call(finish, out_shape=[jax.ShapeDtypeStruct((HEADS, WIDTH, TOK...]
where the time goes in v4:
time: 55.6 us; the launch traced here: 55.4 us
  Pallas kernels  54.6 us (98%)
  between operations  0.8 us (1%)
    pallas_call x1, Pallas kernels, local(): pl.pallas_call(kernel, out_shape=[jax.ShapeDtypeStruct((HEADS, WIDTH, TOK...  52.3 us
    pallas_call x1, Pallas kernels, local(): pl.pallas_call(finish, out_shape=[jax.ShapeDtypeStruct((HEADS, WIDTH, TOK...  2.36 us

profile of v4, /device:TPU:0, one launch (start us, length us, event | category | flops | bytes accessed | tf_op | source)
XLA Modules:
  0.0 55.4 jit_solution(4654030290454422738)
XLA Ops:
  0.6 52.3 %latent_attention_backward.1 = (bf16[8,576,128]{2,1,0:T(8,128)(2,1)}, bf16[8,80,128]{2,1,0:T(8,128)(2,1)}) custom-call(bf16[576,128]{1,0:T(8,128)(2,1)} %bitcast.9, s32[1,128]{1,0:T(1,128)} %bitcast.11, s32[16,128]{1,0:T(8,128)} %bitcast.10, bf16[8,576,128]{2,1,0:T(8,128)(2,1)} %bitcast.7, bf16[1024,512]{1,0:T(8,128)(2,1)} %bitcast.8), custom_call_target="tpu_custom_call" | custom-call | tf_op jit(solution)/shard_map/latent_attention_backward/pallas_call | solution.py:433
  52.9 2.4 %finish.1 = (bf16[8,576,128]{2,1,0:T(8,128)(2,1)}, bf16[576,128]{1,0:T(8,128)(2,1)}) custom-call(bf16[8,576,128]{2,1,0:T(8,128)(2,1)} %get-tuple-element.6.d_query, bf16[8,80,128]{2,1,0:T(8,128)(2,1)} %get-tuple-element.7.pieces, s32[1,128]{1,0:T(1,128)} %bitcast.12), custom_call_target="tpu_custom_call" | custom-call | tf_op jit(solution)/shard_map/finish/pallas_call | solution.py:490

commit v5 on v4

--- a/solution.py
+++ b/solution.py
@@ -329,9 +329,9 @@
     store = pltpu.make_async_copy(q_in, d_query, in_sem.at[2])
     store.start()
 
-    for copy in x_step:
-        copy.wait_recv()
     for half in range(2):
+        for copy in x_step[3 * half : 3 * half + 3]:
+            copy.wait_recv()
         size, first_row = X_SIZES[half], half * X_SIZES[0]
         for g in range(8):
             total = chip[2 * half][core, g, rows_of(x, size), :].astype(F32)
@@ -347,9 +347,9 @@
         copy = remote(source, x_last.at[k], xl_send.at[k], xl_got.at[k], device)
         copy.start()
         x_end.append(copy)
-    for copy in y_step:
-        copy.wait_recv()
     for half in range(2):
+        for copy in y_step[7 * half : 7 * half + 7]:
+            copy.wait_recv()
         total = chip[2 * half + 1][core, group].astype(F32)
         for k in range(7):
             total = total + y_recv[half][k].astype(F32)

time: 55.6 us -> 55.5 us (level)
  no operation moved by 1% of the time
where the time goes in v5:
time: 55.5 us; the launch traced here: 55.4 us
  Pallas kernels  54.6 us (98%)
  between operations  0.8 us (1%)
    pallas_call x1, Pallas kernels, local(): pl.pallas_call(kernel, out_shape=[jax.ShapeDtypeStruct((HEADS, WIDTH, TOK...  52.2 us
    pallas_call x1, Pallas kernels, local(): pl.pallas_call(finish, out_shape=[jax.ShapeDtypeStruct((HEADS, WIDTH, TOK...  2.36 us

profile of v5, /device:TPU:0, one launch (start us, length us, event | category | flops | bytes accessed | tf_op | source)
XLA Modules:
  0.0 55.4 jit_solution(4686005504525535589)
XLA Ops:
  0.6 52.2 %latent_attention_backward.1 = (bf16[8,576,128]{2,1,0:T(8,128)(2,1)}, bf16[8,80,128]{2,1,0:T(8,128)(2,1)}) custom-call(bf16[576,128]{1,0:T(8,128)(2,1)} %bitcast.9, s32[1,128]{1,0:T(1,128)} %bitcast.11, s32[16,128]{1,0:T(8,128)} %bitcast.10, bf16[8,576,128]{2,1,0:T(8,128)(2,1)} %bitcast.7, bf16[1024,512]{1,0:T(8,128)(2,1)} %bitcast.8), custom_call_target="tpu_custom_call" | custom-call | tf_op jit(solution)/shard_map/latent_attention_backward/pallas_call | solution.py:433
  52.9 2.4 %finish.1 = (bf16[8,576,128]{2,1,0:T(8,128)(2,1)}, bf16[576,128]{1,0:T(8,128)(2,1)}) custom-call(bf16[8,576,128]{2,1,0:T(8,128)(2,1)} %get-tuple-element.6.d_query, bf16[8,80,128]{2,1,0:T(8,128)(2,1)} %get-tuple-element.7.pieces, s32[1,128]{1,0:T(1,128)} %bitcast.12), custom_call_target="tpu_custom_call" | custom-call | tf_op jit(solution)/shard_map/finish/pallas_call | solution.py:490

commit v6 on v4

--- a/solution.py
+++ b/solution.py
@@ -83,7 +83,7 @@
         pltpu.make_async_copy(d_out, g_in, in_sem.at[2]),
         pltpu.make_async_copy(docs, docs_in, in_sem.at[4]),
     ]
-    for copy in loads:
+    for copy in loads[:2]:
         copy.start()
     loads[0].wait()
     loads[1].wait()
@@ -108,6 +108,8 @@
         small.append(copy)
     to_twin = [remote(blocks.at[me], blocks.at[me], c_send.at[28], c_recv.at[28], twin)]
     to_twin[0].start()
+    for copy in loads[2:]:
+        copy.start()
 
     loads[2].wait()
     for h in range(HEADS):

time: 55.6 us -> 55.6 us (level)
  no operation moved by 1% of the time
where the time goes in v6:
time: 55.6 us; the launch traced here: 55.4 us
  Pallas kernels  54.6 us (98%)
  between operations  0.8 us (1%)
    pallas_call x1, Pallas kernels, local(): pl.pallas_call(kernel, out_shape=[jax.ShapeDtypeStruct((HEADS, WIDTH, TOK...  52.3 us
    pallas_call x1, Pallas kernels, local(): pl.pallas_call(finish, out_shape=[jax.ShapeDtypeStruct((HEADS, WIDTH, TOK...  2.36 us

profile of v6, /device:TPU:0, one launch (start us, length us, event | category | flops | bytes accessed | tf_op | source)
XLA Modules:
  0.0 55.4 jit_solution(14551595306394216182)
XLA Ops:
  0.6 52.3 %latent_attention_backward.1 = (bf16[8,576,128]{2,1,0:T(8,128)(2,1)}, bf16[8,80,128]{2,1,0:T(8,128)(2,1)}) custom-call(bf16[576,128]{1,0:T(8,128)(2,1)} %bitcast.9, s32[1,128]{1,0:T(1,128)} %bitcast.11, s32[16,128]{1,0:T(8,128)} %bitcast.10, bf16[8,576,128]{2,1,0:T(8,128)(2,1)} %bitcast.7, bf16[1024,512]{1,0:T(8,128)(2,1)} %bitcast.8), custom_call_target="tpu_custom_call" | custom-call | tf_op jit(solution)/shard_map/latent_attention_backward/pallas_call | solution.py:435
  52.9 2.4 %finish.1 = (bf16[8,576,128]{2,1,0:T(8,128)(2,1)}, bf16[576,128]{1,0:T(8,128)(2,1)}) custom-call(bf16[8,576,128]{2,1,0:T(8,128)(2,1)} %get-tuple-element.6.d_query, bf16[8,80,128]{2,1,0:T(8,128)(2,1)} %get-tuple-element.7.pieces, s32[1,128]{1,0:T(1,128)} %bitcast.12), custom_call_target="tpu_custom_call" | custom-call | tf_op jit(solution)/shard_map/finish/pallas_call | solution.py:492
